TPU v7x, 128 devices: a whole 4x4x4 slice. The times are simulated.
128 devices in a mesh: grp: 4 (over y_lo, core), slab: 32 (over z, x, y_hi).
Axes of the slice: x: 4, y: 4 (y_hi: 2, y_lo: 2; y = y_hi * 2 + y_lo), z: 4, core: 2. Of those that a mesh axis runs over, the one named last changes fastest.
Arguments:
- velocity: float32 [3, 128, 144, 512], P(None, 'slab', None, 'grp'), may hold values from -6 to 6
- w_in: bfloat16 [27, 16, 3], replicated, may hold values from -0.625 to 0.625
- w_mid_a: bfloat16 [27, 16, 16], replicated, may hold values from -0.3125 to 0.3125
- w_mid_b: bfloat16 [27, 16, 16], replicated, may hold values from -0.3125 to 0.3125
- w_out: bfloat16 [27, 6, 16], replicated, may hold values from -0.3125 to 0.3125
Outputs:
- velocity_next: float32 [3, 128, 144, 512], P(None, 'slab', None, 'grp')
- stress: bfloat16 [6, 64, 72, 256], P(None, 'slab', 'grp')
- grad_in: float32 [27, 16, 3], replicated
- grad_mid_a: float32 [27, 16, 16], replicated
- grad_mid_b: float32 [27, 16, 16], replicated
- grad_out: float32 [27, 6, 16], replicated
All inputs are finite; a program needn't handle non-finite values.
Results may differ from a plain program's by a relative error of at most 0.0071.
Values may be sent and summed in bfloat16 or wider, within the bound.
A program may use at most 448 MiB of HBM per device.

v0:
```python
import jax
import jax.numpy as jnp
from jax import lax
from jax.sharding import PartitionSpec as P

step_size = 0.1
viscosity = 0.5
closure_weight = 4.0
pair_table = ((0, 3, 4), (3, 1, 5), (4, 5, 2))
stress_pairs = ((0, 0), (1, 1), (2, 2), (0, 1), (0, 2), (1, 2))


def with_halo(cells, sides, width):
    for axis, dim in sides:
        count = lax.axis_size(axis)
        head = lax.slice_in_dim(cells, 0, width, axis=dim)
        tail = lax.slice_in_dim(cells, cells.shape[dim] - width, cells.shape[dim], axis=dim)
        cells = jnp.concatenate(
            [
                lax.ppermute(tail, axis, [(i, (i + 1) % count) for i in range(count)]),
                cells,
                lax.ppermute(head, axis, [((i + 1) % count, i) for i in range(count)]),
            ],
            axis=dim,
        )
    return cells


def gradient_along(padded, along):
    length = padded.shape[along] - 4

    def window_at(offset):
        return lax.slice_in_dim(padded, offset, offset + length, axis=along)

    return (window_at(0) - 8.0 * window_at(1) + 8.0 * window_at(3) - window_at(4)) / 12.0


def laplace_along(padded, along):
    length = padded.shape[along] - 4

    def window_at(offset):
        return lax.slice_in_dim(padded, offset, offset + length, axis=along)

    return (
        -window_at(0)
        + 16.0 * window_at(1)
        - 30.0 * window_at(2)
        + 16.0 * window_at(3)
        - window_at(4)
    ) / 12.0


def wall_ghosts(interior):
    return jnp.pad(interior, ((0, 0), (0, 0), (2, 2), (0, 0)))


def stress_force(extended):
    inner_x = extended[:, :, :, 2:-2]
    inner_z = extended[:, 2:-2]
    walled = wall_ghosts(extended[:, 2:-2, :, 2:-2])
    components = []
    for along_x, along_y, along_z in pair_table:
        summed = gradient_along(inner_x[along_x : along_x + 1], 1)
        summed = summed + gradient_along(walled[along_y : along_y + 1], 2)
        summed = summed + gradient_along(inner_z[along_z : along_z + 1], 3)
        components.append(-closure_weight * summed)
    return jnp.concatenate(components, axis=0)


def tendency(extended, forcing):
    inner_x = extended[:, :, :, 2:-2]
    inner_z = extended[:, 2:-2]
    interior = extended[:, 2:-2, :, 2:-2]
    walled = wall_ghosts(interior)
    advect = interior[0:1] * gradient_along(inner_x, 1)
    advect = advect + interior[1:2] * gradient_along(walled, 2)
    advect = advect + interior[2:3] * gradient_along(inner_z, 3)
    diffuse = laplace_along(inner_x, 1) + laplace_along(walled, 2) + laplace_along(inner_z, 3)
    return -advect + viscosity * diffuse + forcing


def block_mean(field):
    comps, cells_x, cells_y, cells_z = field.shape
    return field.reshape(comps, cells_x // 2, 2, cells_y // 2, 2, cells_z // 2, 2).mean(
        axis=(2, 4, 6)
    )


def filter_fields(velocity):
    block_means = block_mean(velocity)
    products = jnp.stack(
        [velocity[left_comp] * velocity[right_comp] for left_comp, right_comp in stress_pairs]
    )
    resolved = jnp.stack(
        [block_means[left_comp] * block_means[right_comp] for left_comp, right_comp in stress_pairs]
    )
    return jnp.concatenate([block_means, block_mean(products) - resolved], axis=0).astype(
        jnp.bfloat16
    )


def prolong(coarse):
    return jnp.repeat(jnp.repeat(jnp.repeat(coarse, 2, axis=1), 2, axis=2), 2, axis=3)


def extend_depth(activation):
    rimmed = with_halo(activation, (("grp", 2), ("slab", 1)), 1)
    place = lax.axis_index("grp")
    count = lax.axis_size("grp")
    rows = jnp.arange(rimmed.shape[2])
    keep = ((rows > 0) | (place > 0)) & ((rows < rimmed.shape[2] - 1) | (place < count - 1))
    return rimmed * keep[None, None, :, None].astype(rimmed.dtype)


def shifted_stack(padded):
    in_ch = padded.shape[0]
    outer_rows = padded.shape[1] - 2
    middle_rows = padded.shape[2] - 2
    stacked = jnp.stack(
        [
            padded[:, shift_a : shift_a + outer_rows, shift_b : shift_b + middle_rows, :]
            for shift_a in range(3)
            for shift_b in range(3)
        ]
    )
    return stacked.reshape(9 * in_ch, outer_rows * middle_rows * padded.shape[3])


def convolve(padded, weight):
    out_ch, in_ch = (weight.shape[1], weight.shape[2])
    outer_rows = padded.shape[1] - 2
    middle_rows = padded.shape[2] - 2
    inner_rows = padded.shape[3]
    columns = shifted_stack(padded)
    kernel = weight.reshape(3, 3, 3, out_ch, in_ch)
    summed = jnp.zeros((out_ch, outer_rows, middle_rows, inner_rows), jnp.float32)
    for shift_z in range(3):
        flat_kernel = jnp.transpose(kernel[:, :, shift_z], (2, 0, 1, 3)).reshape(out_ch, 9 * in_ch)
        partial_value = jnp.dot(flat_kernel, columns, preferred_element_type=jnp.float32)
        partial_value = partial_value.reshape(out_ch, outer_rows, middle_rows, inner_rows)
        summed = summed + jnp.roll(partial_value, 1 - shift_z, axis=3)
    return summed


def weight_gradient(cotangent, padded):
    out_ch = cotangent.shape[0]
    in_ch = padded.shape[0]
    columns = shifted_stack(padded)
    partials = []
    for shift_z in range(3):
        moved = jnp.roll(cotangent, shift_z - 1, axis=3).reshape(out_ch, columns.shape[1])
        partial_value = lax.dot_general(
            moved, columns, (((1,), (1,)), ((), ())), preferred_element_type=jnp.float32
        )
        partials.append(jnp.transpose(partial_value.reshape(out_ch, 3, 3, in_ch), (1, 2, 0, 3)))
    return jnp.stack(partials, axis=2).reshape(27, out_ch, in_ch)


def flip_weight(weight):
    out_ch, in_ch = (weight.shape[1], weight.shape[2])
    kernel = weight.reshape(3, 3, 3, out_ch, in_ch)[::-1, ::-1, ::-1]
    return jnp.transpose(kernel, (0, 1, 2, 4, 3)).reshape(27, in_ch, out_ch)


def advance(velocity, stress_x):
    rimmed = with_halo(stress_x, (("grp", 3), ("slab", 1)), 2)
    forcing = stress_force(prolong(rimmed.astype(jnp.float32)))
    extended = with_halo(velocity.astype(jnp.bfloat16), (("grp", 3), ("slab", 1)), 4).astype(
        velocity.dtype
    )
    first_section = extended[:, 2:-2, :, 2:-2] + step_size * tendency(extended, forcing)
    second = tendency(first_section, forcing[:, 2:-2, :, 2:-2])
    return 0.5 * (velocity + first_section[:, 2:-2, :, 2:-2] + step_size * second)


def local(velocity, w_in, w_mid_a, w_mid_b, w_out):
    group_count = lax.axis_size("grp")
    slab_count = lax.axis_size("slab")
    fields = filter_fields(velocity)
    relaid = lax.all_to_all(fields, "grp", split_axis=2, concat_axis=3, tiled=True)
    weights = (w_in, w_mid_a, w_mid_b, w_out)
    activation = relaid[:3]
    target = relaid[3:]
    padded_list = []
    response = None
    for layer_index in range(4):
        padded = extend_depth(activation)
        padded_list.append(padded)
        response = convolve(padded, weights[layer_index])
        if layer_index < 3:
            activation = jnp.tanh(response).astype(jnp.bfloat16)
    stress = response.astype(jnp.bfloat16)
    stress_x = lax.all_to_all(stress, "grp", split_axis=3, concat_axis=2, tiled=True)
    velocity_next = advance(velocity, stress_x)
    length = (
        6 * response.shape[1] * response.shape[2] * response.shape[3] * group_count * slab_count
    )
    cotangent = (2.0 / length * (response - target.astype(jnp.float32))).astype(jnp.bfloat16)
    gradients = [None, None, None, None]
    for layer_index in (3, 2, 1, 0):
        padded = padded_list[layer_index]
        local_grad = weight_gradient(cotangent, padded)
        gradients[layer_index] = local_grad
        if layer_index > 0:
            spread = convolve(extend_depth(cotangent), flip_weight(weights[layer_index]))
            below_act = padded[:, 1:-1, 1:-1, :].astype(jnp.float32)
            cotangent = (spread * (1.0 - below_act * below_act)).astype(jnp.bfloat16)
    summed = lax.psum((gradients[0], gradients[1], gradients[2], gradients[3]), ("grp", "slab"))
    gradients = list(summed)
    return (velocity_next, stress, gradients[0], gradients[1], gradients[2], gradients[3])


def solution(mesh):
    in_specs = (P(None, "slab", None, "grp"), P(), P(), P(), P())
    out_specs = (P(None, "slab", None, "grp"), P(None, "slab", "grp", None), P(), P(), P(), P())
    return jax.shard_map(local, mesh=mesh, in_specs=in_specs, out_specs=out_specs, check_vma=False)
```

profile of v0, /device:TPU:1, one launch (start us, length us, event | category | flops | bytes accessed | tf_op | source)
XLA Modules:
  0.0 1008.6 jit_solution(5926275811382143952)
XLA Ops:
  7.2 58.8 %reshape.311 = f32[3,2,2,72,2,64,2]{6,5,4,3,2,1,0:T(8,128)} reshape(f32[3,4,144,128]{3,2,1,0:T(8,128)} %param.5) | data formatting | bytes 1769472 | tf_op jit(solution)/shard_map/reshape | solution.py:84
  66.1 17.7 %reduce_sum.18 = f32[3,2,72,64]{3,2,1,0:T(8,128)S(1)} reduce(f32[3,2,2,72,2,64,2]{6,5,4,3,2,1,0:T(8,128)} %reshape.311, f32[]{:T(128)} %constant.54.clone.1), dimensions={2,4,6}, to_apply=%region_0.0 | reduce | flops 193536 | bytes 995332 | tf_op jit(solution)/shard_map/reduce_sum | solution.py:84
  84.0 20.2 %stack.328 = f32[1,2,2,72,2,64,2]{6,5,4,3,2,1,0:T(8,128)} reshape(f32[1,4,144,128]{3,2,1,0:T(8,128)S(1)} %get-tuple-element.56) | data formatting | bytes 589824 | tf_op jit(solution)/shard_map/stack | solution.py:91
  104.2 13.0 %constant_dynamic-update-slice_fusion.5 = f32[6,2,2,72,2,64,2]{6,5,4,3,2,1,0:T(8,128)} fusion(f32[1,2,2,72,2,64,2]{6,5,4,3,2,1,0:T(8,128)} %stack.328), kind=kLoop, calls=%fused_computation.291 | loop fusion | bytes 19169280
  117.3 20.2 %stack.329 = f32[1,2,2,72,2,64,2]{6,5,4,3,2,1,0:T(8,128)} reshape(f32[1,4,144,128]{3,2,1,0:T(8,128)S(1)} %get-tuple-element.57) | data formatting | bytes 589824 | tf_op jit(solution)/shard_map/stack | solution.py:91
  137.5 20.2 %stack.330 = f32[1,2,2,72,2,64,2]{6,5,4,3,2,1,0:T(8,128)} reshape(f32[1,4,144,128]{3,2,1,0:T(8,128)S(1)} %get-tuple-element.58) | data formatting | bytes 589824 | tf_op jit(solution)/shard_map/stack | solution.py:91
  157.7 20.2 %stack.331 = f32[1,2,2,72,2,64,2]{6,5,4,3,2,1,0:T(8,128)} reshape(f32[1,4,144,128]{3,2,1,0:T(8,128)S(1)} %get-tuple-element.54) | data formatting | bytes 589824 | tf_op jit(solution)/shard_map/stack | solution.py:91
  177.8 20.2 %stack.332 = f32[1,2,2,72,2,64,2]{6,5,4,3,2,1,0:T(8,128)} reshape(f32[1,4,144,128]{3,2,1,0:T(8,128)S(1)} %get-tuple-element.55) | data formatting | bytes 589824 | tf_op jit(solution)/shard_map/stack | solution.py:91
  198.1 20.2 %stack.333 = f32[1,2,2,72,2,64,2]{6,5,4,3,2,1,0:T(8,128)} reshape(f32[1,4,144,128]{3,2,1,0:T(8,128)S(1)} %get-tuple-element.53) | data formatting | bytes 589824 | tf_op jit(solution)/shard_map/stack | solution.py:91
  218.2 13.1 %constant_dynamic-update-slice_fusion.4 = f32[6,2,2,72,2,64,2]{6,5,4,3,2,1,0:T(8,128)} fusion(f32[6,2,2,72,2,64,2]{6,5,4,3,2,1,0:T(8,128)} %constant_dynamic-update-slice_fusion.5, f32[1,2,2,72,2,64,2]{6,5,4,3,2,1,0:T(8,128)} %stack.329), kind=kLoop, calls=%fused_computation.290 | loop fusion | bytes 37748736
  231.3 15.2 %constant_dynamic-update-slice_fusion.3 = f32[6,2,2,72,2,64,2]{6,5,4,3,2,1,0:T(8,128)} fusion(f32[6,2,2,72,2,64,2]{6,5,4,3,2,1,0:T(8,128)} %constant_dynamic-update-slice_fusion.4, f32[1,2,2,72,2,64,2]{6,5,4,3,2,1,0:T(8,128)} %stack.330), kind=kLoop, calls=%fused_computation.289 | loop fusion | bytes 37748736
  246.5 15.5 %constant_dynamic-update-slice_fusion.2 = f32[6,2,2,72,2,64,2]{6,5,4,3,2,1,0:T(8,128)} fusion(f32[6,2,2,72,2,64,2]{6,5,4,3,2,1,0:T(8,128)} %constant_dynamic-update-slice_fusion.3, f32[1,2,2,72,2,64,2]{6,5,4,3,2,1,0:T(8,128)} %stack.331), kind=kLoop, calls=%fused_computation.288 | loop fusion | bytes 37748736
  262.0 10.0 constant_dynamic-update-slice_fusion.1
  273.8 7.9 constant_dynamic-update-slice_fusion
  281.7 34.5 %reduce_sum.19 = f32[6,2,72,64]{3,2,1,0:T(8,128)S(1)} reduce(f32[6,2,2,72,2,64,2]{6,5,4,3,2,1,0:T(8,128)} %constant_dynamic-update-slice_fusion, f32[]{:T(128)} %constant.54.clone.1), dimensions={2,4,6}, to_apply=%region_1.0 | reduce | flops 387072 | bytes 1990660 | tf_op jit(solution)/shard_map/reduce_sum | solution.py:84
  317.6 4.9 all-to-all-start
  335.7 3.1 collective-permute-start.6
  338.8 5.7 collective-permute-start.7
  365.4 7.3 collective-permute-start.11
  373.3 4.5 collective-permute-done.10
  386.1 4.5 reshape.320
  410.8 7.2 collective-permute-start.3
  418.4 7.2 collective-permute-start.15
  428.9 5.5 dot_general.195
  434.4 19.4 %collective-permute-done.14 = bf16[16,1,20,256]{3,2,1,0:T(8,128)(2,1)S(1)} collective-permute-done((bf16[16,1,20,256]{3,2,1,0:T(8,128)(2,1)S(1)}, bf16[16,1,20,256]{3,2,1,0:T(8,128)(2,1)S(1)}, u32[]{:S(2)}, u32[]{:S(2)}) %collective-permute-start.14) | collective-permute-done | bytes 163872 | tf_op jit(solution)/shard_map/ppermute | solution.py:20
  453.8 3.4 collective-permute-done.15
  465.4 4.1 reshape.328
  486.8 3.9 collective-permute-start.16
  495.2 6.7 collective-permute-start.19
  505.8 5.5 dot_general.199
  519.5 4.1 reshape.336
  540.7 4.1 dot_general.203
  556.6 4.0 convolution_bitcast_fusion.29
  564.7 3.0 convolution_bitcast_fusion.28
  570.5 7.2 collective-permute-start.27
  580.3 4.3 all-to-all-start.1
  604.2 4.6 convolution_bitcast_fusion.23
  608.8 3.6 convolution_bitcast_fusion.22
  612.9 3.0 convolution_bitcast_fusion.21
  624.6 9.0 collective-permute-done.20
  633.9 7.2 collective-permute-start.23
  641.9 7.2 collective-permute-start.31
  649.5 4.1 broadcast_in_dim.7
  653.6 6.7 copy.258
  660.3 10.1 %broadcast_in_dim.8 = f32[6,12,144,68,2]{2,4,3,1,0:T(2,128)} broadcast(f32[6,12,144,68]{2,3,1,0:T(8,128)} %copy.258), dimensions={0,1,2,3} | broadcast | bytes 8460288 | tf_op jit(solution)/shard_map/broadcast_in_dim | solution.py:103
  670.5 12.7 %reshape.346 = f32[6,12,144,136]{2,3,1,0:T(8,128)} reshape(f32[6,12,144,68,2]{2,4,3,1,0:T(2,128)} %broadcast_in_dim.8) | data formatting | bytes 11280384 | tf_op jit(solution)/shard_map/reshape | solution.py:103
  683.2 3.6 slice.1249
  691.3 3.9 fusion.13
  695.2 14.0 %fusion.2 = (f32[3,8,144,132]{2,3,1,0:T(8,128)S(1)}, f32[3,8,144,132]{2,3,1,0:T(8,128)}) fusion(f32[3,8,144,132]{2,3,1,0:T(8,128)} %slice.1147, f32[3,12,144,136]{2,3,1,0:T(8,128)S(1)} %bitcast.598, f32[8,144,132]{1,2,0:T(8,128)} %get-tuple-element.46, f32[8,144,132]{1,2,0:T(8,128)} %get-tuple-element.47, f32[8,144,132]{1,2,0:T(8,128)} %get-tuple-element.45, ...), kind=kLoop, calls=%fused_computation.25 | loop fusion | flops 23721984 | bytes 23721984 | tf_op jit(solution)/shard_map/add | solution.py:171
  721.0 5.7 reshape.354
  726.7 3.1 convolution_bitcast_fusion.3
  735.9 3.1 convolution_bitcast_fusion.5
  743.0 3.1 convolution_bitcast_fusion.4
  759.7 5.6 convolution_bitcast_fusion.26
  765.3 4.6 convolution_bitcast_fusion.25
  769.9 3.6 collective-permute-start.32
  778.6 7.2 collective-permute-start.35
  785.8 4.8 convolution_bitcast_fusion.24
  800.3 5.7 reshape.361
  806.1 3.1 convolution_bitcast_fusion
  815.3 3.1 convolution_bitcast_fusion.2
  822.3 3.1 convolution_bitcast_fusion.1
  847.9 8.5 fusion.7
  859.2 135.5 %all-reduce.6.cloned.1.call-done = (f32[27,16,3]{1,0,2:T(8,128)}, f32[27,16,16]{2,1,0:T(8,128)}, f32[27,16,16]{2,1,0:T(8,128)}, f32[27,6,16]{2,1,0:T(8,128)}) async-done(((f32[27,16,3]{1,0,2:T(8,128)}, f32[27,16,16]{2,1,0:T(8,128)}, f32[27,16,16]{2,1,0:T(8,128)}, f32[27,6,16]{2,1,0:T(8,128)}), (f32[27,16,3]{1,0,2:T(8,128)}, f32[27,16,16]{2,1,0:T(8,128)}, f32[27,16,16]{2,1,0:T(8,128)}, ...) | async-done | bytes 70864 | tf_op jit(solution)/shard_map/psum | solution.py:208
  (512 shorter events, 276.5 us)
Async XLA Ops:
  7.2 58.8 %copy-start.13 = (f32[3,4,144,128]{3,2,1,0:T(8,128)S(1)}, f32[3,4,144,128]{3,2,1,0:T(8,128)}, u32[]{:S(2)}) copy-start(f32[3,4,144,128]{3,2,1,0:T(8,128)} %param.5) | copy-start | bytes 2654212
  231.3 30.7 %slice-start.2 = ((s8[18874368]{0:T(1024)(128)(4,1)}), s8[4194304]{0:T(1024)(128)(4,1)S(1)}, s32[]{:S(2)}) async-start(s8[18874368]{0:T(1024)(128)(4,1)} %bitcast.599), calls=%async_computation.5 | async-start | bytes 8388608
  231.3 30.7 %slice-start.3 = ((s8[18874368]{0:T(1024)(128)(4,1)}), s8[4194304]{0:T(1024)(128)(4,1)S(1)}, s32[]{:S(2)}) async-start(s8[18874368]{0:T(1024)(128)(4,1)} %bitcast.599), calls=%async_computation.6 | async-start | bytes 8388608
  231.3 30.7 %slice-start.4 = ((s8[18874368]{0:T(1024)(128)(4,1)}), s8[4194304]{0:T(1024)(128)(4,1)S(1)}, s32[]{:S(2)}) async-start(s8[18874368]{0:T(1024)(128)(4,1)} %bitcast.599), calls=%async_computation.7 | async-start | bytes 8388608
  246.5 15.5 %slice-start.5 = ((s8[18874368]{0:T(1024)(128)(4,1)}), s8[4194304]{0:T(1024)(128)(4,1)S(1)}, s32[]{:S(2)}) async-start(s8[18874368]{0:T(1024)(128)(4,1)} %bitcast.599), calls=%async_computation.8 | async-start | bytes 8388608
  246.5 15.5 %slice-start.6 = ((s8[18874368]{0:T(1024)(128)(4,1)}), s8[2097152]{0:T(1024)(128)(4,1)S(1)}, s32[]{:S(2)}) async-start(s8[18874368]{0:T(1024)(128)(4,1)} %bitcast.599), calls=%async_computation.9 | async-start | bytes 4194304
  246.5 25.6 %slice-start.7 = ((s8[18874368]{0:T(1024)(128)(4,1)}), s8[4194304]{0:T(1024)(128)(4,1)S(1)}, s32[]{:S(2)}) async-start(s8[18874368]{0:T(1024)(128)(4,1)} %bitcast.601), calls=%async_computation.10 | async-start | bytes 8388608
  246.5 25.6 %slice-start.8 = ((s8[18874368]{0:T(1024)(128)(4,1)}), s8[4194304]{0:T(1024)(128)(4,1)S(1)}, s32[]{:S(2)}) async-start(s8[18874368]{0:T(1024)(128)(4,1)} %bitcast.601), calls=%async_computation.11 | async-start | bytes 8388608
  246.5 25.6 %slice-start.9 = ((s8[18874368]{0:T(1024)(128)(4,1)}), s8[4194304]{0:T(1024)(128)(4,1)S(1)}, s32[]{:S(2)}) async-start(s8[18874368]{0:T(1024)(128)(4,1)} %bitcast.601), calls=%async_computation.12 | async-start | bytes 8388608
  262.0 11.2 %slice-start.10 = ((s8[18874368]{0:T(1024)(128)(4,1)}), s8[4194304]{0:T(1024)(128)(4,1)S(1)}, s32[]{:S(2)}) async-start(s8[18874368]{0:T(1024)(128)(4,1)} %bitcast.601), calls=%async_computation.13 | async-start | bytes 8388608
  262.0 11.8 %slice-start.11 = ((s8[18874368]{0:T(1024)(128)(4,1)}), s8[2097152]{0:T(1024)(128)(4,1)S(1)}, s32[]{:S(2)}) async-start(s8[18874368]{0:T(1024)(128)(4,1)} %bitcast.601), calls=%async_computation.14 | async-start | bytes 4194304
  317.6 12.5 %all-to-all-start = ((bf16[4,2,10368]{2,1,0:T(2,128)(2,1)}), bf16[4,2,10368]{2,1,0:T(2,128)(2,1)S(1)}, u32[]{:S(2)}, u32[]{:S(2)}) async-start(bf16[4,2,10368]{2,1,0:T(2,128)(2,1)} %reshape.410), calls=%async_computation | async-start | bytes 331776 | tf_op jit(solution)/shard_map/all_to_all | solution.py:180
  323.9 85.0 %collective-permute-start = (bf16[3,4,144,4]{2,3,1,0:T(4,128)(2,1)}, bf16[3,4,144,4]{2,3,1,0:T(4,128)(2,1)}, u32[]{:S(2)}, u32[]{:S(2)}) collective-permute-start(bf16[3,4,144,4]{2,3,1,0:T(4,128)(2,1)} %get-tuple-element.59), channel_id=1, source_target_pairs={{0,32},{32,64},{64,96},{96,0},{1,33},{33,65},{65,97},{97,1},{2,34}... | collective-permute-start | bytes 41480 | tf_op jit(solution)/shard_map/ppermute | solution.py:20
  325.5 83.4 %collective-permute-start.1 = (bf16[3,4,144,4]{2,3,1,0:T(4,128)(2,1)}, bf16[3,4,144,4]{2,3,1,0:T(4,128)(2,1)}, u32[]{:S(2)}, u32[]{:S(2)}) collective-permute-start(bf16[3,4,144,4]{2,3,1,0:T(4,128)(2,1)} %get-tuple-element.60), channel_id=1, source_target_pairs={{32,0},{64,32},{96,64},{0,96},{33,1},{65,33},{97,65},{1,97},{34,2}... | collective-permute-start | bytes 41480 | tf_op jit(solution)/shard_map/ppermute | solution.py:22
  330.5 16.7 %copy-start.29 = (bf16[9,2,4,18,64]{4,2,3,1,0:T(4,128)(2,1)}, bf16[9,2,4,18,64]{4,2,3,1,0:T(4,128)(2,1)S(1)}, u32[]{:S(2)}) copy-start(bf16[9,2,4,18,64]{4,2,3,1,0:T(4,128)(2,1)S(1)} %copy.320) | copy-start | bytes 497668
  330.7 2.6 collective-permute-start.4
  332.5 3.1 collective-permute-start.5
  335.7 10.4 %collective-permute-start.6 = (bf16[3,1,20,256]{3,1,2,0:T(2,128)(2,1)S(1)}, bf16[3,1,20,256]{3,1,2,0:T(2,128)(2,1)S(1)}, u32[]{:S(2)}, u32[]{:S(2)}) collective-permute-start(bf16[3,1,20,256]{3,1,2,0:T(2,128)(2,1)S(1)} %get-tuple-element.117), channel_id=1, source_target_pairs={{0,1},{1,2},{2,3},{3,4},{4,5},{5,6},{6,7},{7,8},{8,9},{9,10},{10,1... | collective-permute-start | bytes 92168 | tf_op jit(solution)/shard_map/ppermute | solution.py:20
  338.8 7.4 collective-permute-start.7
  357.3 7.1 collective-permute-start.8
  357.7 6.7 collective-permute-start.9
  364.7 13.1 %collective-permute-start.10 = (bf16[16,1,20,256]{3,2,1,0:T(8,128)(2,1)S(1)}, bf16[16,1,20,256]{3,2,1,0:T(8,128)(2,1)S(1)}, u32[]{:S(2)}, u32[]{:S(2)}) collective-permute-start(bf16[16,1,20,256]{3,2,1,0:T(8,128)(2,1)S(1)} %get-tuple-element.89), channel_id=1, source_target_pairs={{0,1},{1,2},{2,3},{3,4},{4,5},{5,6},{6,7},{7,8},{8,9},{9,10},{10,1... | collective-permute-start | bytes 491528 | tf_op jit(solution)/shard_map/ppermute | solution.py:20
  365.4 12.4 %collective-permute-start.11 = (bf16[16,1,20,256]{3,2,1,0:T(8,128)(2,1)S(1)}, bf16[16,1,20,256]{3,2,1,0:T(8,128)(2,1)S(1)}, u32[]{:S(2)}, u32[]{:S(2)}) collective-permute-start(bf16[16,1,20,256]{3,2,1,0:T(8,128)(2,1)S(1)} %get-tuple-element.90), channel_id=1, source_target_pairs={{1,0},{2,1},{3,2},{4,3},{5,4},{6,5},{7,6},{8,7},{9,8},{10,9},{11,1... | collective-permute-start | bytes 491528 | tf_op jit(solution)/shard_map/ppermute | solution.py:22
  405.9 19.7 %copy-start.30 = (bf16[9,2,4,18,64]{4,2,3,1,0:T(4,128)(2,1)S(1)}, bf16[9,2,4,18,64]{4,2,3,1,0:T(4,128)(2,1)}, u32[]{:S(2)}) copy-start(bf16[9,2,4,18,64]{4,2,3,1,0:T(4,128)(2,1)} %copy-done.29) | copy-start | bytes 497668
  408.0 10.0 collective-permute-start.12
  408.4 19.3 %copy-start.16 = (bf16[9,3,2,18,256]{4,3,2,1,0:T(8,128)(2,1)S(1)}, bf16[9,3,2,18,256]{4,3,2,1,0:T(8,128)(2,1)}, u32[]{:S(2)}) copy-start(bf16[9,3,2,18,256]{4,3,2,1,0:T(8,128)(2,1)} %copy-done.15) | copy-start | bytes 1492996
  408.4 9.6 collective-permute-start.13
  410.8 80.2 %collective-permute-start.2 = (bf16[3,4,144,136]{2,3,1,0:T(8,128)(2,1)}, bf16[3,4,144,136]{2,3,1,0:T(8,128)(2,1)}, u32[]{:S(2)}, u32[]{:S(2)}) collective-permute-start(bf16[3,4,144,136]{2,3,1,0:T(8,128)(2,1)} %pad_maximum_fusion.1), channel_id=1, source_target_pairs={{0,1},{1,2},{2,3},{3,4},{4,5},{5,6},{6,7},{7,8},{8,9},{9,10},{10,1... | collective-permute-start | bytes 1410056 | tf_op jit(solution)/shard_map/ppermute | solution.py:20
  410.8 80.2 %collective-permute-start.3 = (bf16[3,4,144,136]{2,3,1,0:T(8,128)(2,1)}, bf16[3,4,144,136]{2,3,1,0:T(8,128)(2,1)}, u32[]{:S(2)}, u32[]{:S(2)}) collective-permute-start(bf16[3,4,144,136]{2,3,1,0:T(8,128)(2,1)} %pad_maximum_fusion.1), channel_id=1, source_target_pairs={{1,0},{2,1},{3,2},{4,3},{5,4},{6,5},{7,6},{8,7},{9,8},{10,9},{11,1... | collective-permute-start | bytes 1410056 | tf_op jit(solution)/shard_map/ppermute | solution.py:22
  418.3 35.5 %collective-permute-start.14 = (bf16[16,1,20,256]{3,2,1,0:T(8,128)(2,1)S(1)}, bf16[16,1,20,256]{3,2,1,0:T(8,128)(2,1)S(1)}, u32[]{:S(2)}, u32[]{:S(2)}) collective-permute-start(bf16[16,1,20,256]{3,2,1,0:T(8,128)(2,1)S(1)} %get-tuple-element.85), channel_id=1, source_target_pairs={{0,1},{1,2},{2,3},{3,4},{4,5},{5,6},{6,7},{7,8},{8,9},{9,10},{10,1... | collective-permute-start | bytes 491528 | tf_op jit(solution)/shard_map/ppermute | solution.py:20
  418.4 38.8 %collective-permute-start.15 = (bf16[16,1,20,256]{3,2,1,0:T(8,128)(2,1)S(1)}, bf16[16,1,20,256]{3,2,1,0:T(8,128)(2,1)S(1)}, u32[]{:S(2)}, u32[]{:S(2)}) collective-permute-start(bf16[16,1,20,256]{3,2,1,0:T(8,128)(2,1)S(1)} %get-tuple-element.86), channel_id=1, source_target_pairs={{1,0},{2,1},{3,2},{4,3},{5,4},{6,5},{7,6},{8,7},{9,8},{10,9},{11,1... | collective-permute-start | bytes 491528 | tf_op jit(solution)/shard_map/ppermute | solution.py:22
  486.8 6.0 collective-permute-start.16
  490.8 3.5 collective-permute-start.17
  492.8 11.1 %copy-start = (f32[3,12,144,136]{2,3,1,0:T(8,128)}, f32[3,12,144,136]{2,3,1,0:T(8,128)S(1)}, u32[]{:S(2)}) copy-start(f32[3,12,144,136]{2,3,1,0:T(8,128)S(1)} %maximum_convert_fusion) | copy-start | bytes 8460292
  494.6 16.8 %collective-permute-start.18 = (bf16[16,1,20,256]{3,2,1,0:T(8,128)(2,1)S(1)}, bf16[16,1,20,256]{3,2,1,0:T(8,128)(2,1)S(1)}, u32[]{:S(2)}, u32[]{:S(2)}) collective-permute-start(bf16[16,1,20,256]{3,2,1,0:T(8,128)(2,1)S(1)} %get-tuple-element.81), channel_id=1, source_target_pairs={{0,1},{1,2},{2,3},{3,4},{4,5},{5,6},{6,7},{7,8},{8,9},{9,10},{10,1... | collective-permute-start | bytes 491528 | tf_op jit(solution)/shard_map/ppermute | solution.py:20
  495.2 16.1 %collective-permute-start.19 = (bf16[16,1,20,256]{3,2,1,0:T(8,128)(2,1)S(1)}, bf16[16,1,20,256]{3,2,1,0:T(8,128)(2,1)S(1)}, u32[]{:S(2)}, u32[]{:S(2)}) collective-permute-start(bf16[16,1,20,256]{3,2,1,0:T(8,128)(2,1)S(1)} %get-tuple-element.82), channel_id=1, source_target_pairs={{1,0},{2,1},{3,2},{4,3},{5,4},{6,5},{7,6},{8,7},{9,8},{10,9},{11,1... | collective-permute-start | bytes 491528 | tf_op jit(solution)/shard_map/ppermute | solution.py:22
  563.5 5.9 collective-permute-start.24
  564.3 5.1 collective-permute-start.25
  567.7 16.9 %copy-start.18 = (bf16[6,2,18,256]{3,2,1,0:T(8,128)(2,1)S(1)}, bf16[6,2,18,256]{3,2,1,0:T(8,128)(2,1)}, u32[]{:S(2)}) copy-start(bf16[6,2,18,256]{3,2,1,0:T(8,128)(2,1)} %copy-done.17) | copy-start | bytes 331780
  570.4 14.2 %collective-permute-start.26 = (bf16[6,1,20,256]{3,2,1,0:T(8,128)(2,1)S(1)}, bf16[6,1,20,256]{3,2,1,0:T(8,128)(2,1)S(1)}, u32[]{:S(2)}, u32[]{:S(2)}) collective-permute-start(bf16[6,1,20,256]{3,2,1,0:T(8,128)(2,1)S(1)} %get-tuple-element.101), channel_id=1, source_target_pairs={{0,1},{1,2},{2,3},{3,4},{4,5},{5,6},{6,7},{7,8},{8,9},{9,10},{10,1... | collective-permute-start | bytes 184328 | tf_op jit(solution)/shard_map/ppermute | solution.py:20
  570.5 14.1 %collective-permute-start.27 = (bf16[6,1,20,256]{3,2,1,0:T(8,128)(2,1)S(1)}, bf16[6,1,20,256]{3,2,1,0:T(8,128)(2,1)S(1)}, u32[]{:S(2)}, u32[]{:S(2)}) collective-permute-start(bf16[6,1,20,256]{3,2,1,0:T(8,128)(2,1)S(1)} %get-tuple-element.102), channel_id=1, source_target_pairs={{1,0},{2,1},{3,2},{4,3},{5,4},{6,5},{7,6},{8,7},{9,8},{10,9},{11,1... | collective-permute-start | bytes 184328 | tf_op jit(solution)/shard_map/ppermute | solution.py:22
  580.3 38.9 %all-to-all-start.1 = ((bf16[4,2,6912]{2,1,0:T(2,128)(2,1)}), bf16[4,2,6912]{2,1,0:T(2,128)(2,1)S(1)}, u32[]{:S(2)}, u32[]{:S(2)}) async-start(bf16[4,2,6912]{2,1,0:T(2,128)(2,1)} %reshape.412), calls=%async_computation.1 | async-start | bytes 221184 | tf_op jit(solution)/shard_map/all_to_all | solution.py:193
  584.6 410.1 %all-reduce.6.cloned.1.call-start = ((), (), s32[]{:S(2)}) async-start(), calls=%async_computation.2 | async-start | bytes 1204224 | tf_op jit(solution)/shard_map/psum | solution.py:208
  595.3 8.9 copy-start.3
  604.2 8.3 copy-start.35
  615.8 8.5 copy-start.7
  617.5 6.7 collective-permute-start.28
  619.2 5.1 collective-permute-start.29
  622.3 11.3 %collective-permute-start.20 = (bf16[6,2,72,2]{3,2,1,0:T(8,128)(2,1)S(1)}, bf16[6,2,72,2]{3,2,1,0:T(8,128)(2,1)S(1)}, u32[]{:S(2)}, u32[]{:S(2)}) collective-permute-start(bf16[6,2,72,2]{3,2,1,0:T(8,128)(2,1)S(1)} %get-tuple-element.93), channel_id=1, source_target_pairs={{0,32},{32,64},{64,96},{96,0},{1,33},{33,65},{65,97},{97,1},{2,34}... | collective-permute-start | bytes 10376 | tf_op jit(solution)/shard_map/ppermute | solution.py:20
  624.1 9.5 collective-permute-start.21
  624.3 24.8 %copy-start.52 = (bf16[16,2,1,256]{3,2,1,0:T(2,128)(2,1)}, bf16[16,2,1,256]{3,2,1,0:T(2,128)(2,1)S(1)}, u32[]{:S(2)}) copy-start(bf16[16,2,1,256]{3,2,1,0:T(2,128)(2,1)S(1)} %collective-permute-done.28) | copy-start | bytes 49156
  624.3 24.8 %copy-start.54 = (bf16[16,2,1,256]{3,2,1,0:T(2,128)(2,1)}, bf16[16,2,1,256]{3,2,1,0:T(2,128)(2,1)S(1)}, u32[]{:S(2)}) copy-start(bf16[16,2,1,256]{3,2,1,0:T(2,128)(2,1)S(1)} %collective-permute-done.29) | copy-start | bytes 49156
  633.8 15.2 %collective-permute-start.22 = (bf16[6,2,72,68]{3,2,1,0:T(8,128)(2,1)S(1)}, bf16[6,2,72,68]{3,2,1,0:T(8,128)(2,1)S(1)}, u32[]{:S(2)}, u32[]{:S(2)}) collective-permute-start(bf16[6,2,72,68]{3,2,1,0:T(8,128)(2,1)S(1)} %pad_maximum_fusion.16), channel_id=1, source_target_pairs={{0,1},{1,2},{2,3},{3,4},{4,5},{5,6},{6,7},{7,8},{8,9},{9,10},{10,1... | collective-permute-start | bytes 352520 | tf_op jit(solution)/shard_map/ppermute | solution.py:20
  633.9 15.2 %collective-permute-start.23 = (bf16[6,2,72,68]{3,2,1,0:T(8,128)(2,1)S(1)}, bf16[6,2,72,68]{3,2,1,0:T(8,128)(2,1)S(1)}, u32[]{:S(2)}, u32[]{:S(2)}) collective-permute-start(bf16[6,2,72,68]{3,2,1,0:T(8,128)(2,1)S(1)} %pad_maximum_fusion.16), channel_id=1, source_target_pairs={{1,0},{2,1},{3,2},{4,3},{5,4},{6,5},{7,6},{8,7},{9,8},{10,9},{11,1... | collective-permute-start | bytes 352520 | tf_op jit(solution)/shard_map/ppermute | solution.py:22
  641.9 70.0 %collective-permute-start.30 = (bf16[16,1,20,256]{3,2,1,0:T(8,128)(2,1)}, bf16[16,1,20,256]{3,2,1,0:T(8,128)(2,1)S(1)}, u32[]{:S(2)}, u32[]{:S(2)}) collective-permute-start(bf16[16,1,20,256]{3,2,1,0:T(8,128)(2,1)} %get-tuple-element.77), channel_id=1, source_target_pairs={{0,1},{1,2},{2,3},{3,4},{4,5},{5,6},{6,7},{7,8},{8,9},{9,10},{10,1... | collective-permute-start | bytes 491528 | tf_op jit(solution)/shard_map/ppermute | solution.py:20
  641.9 70.0 %collective-permute-start.31 = (bf16[16,1,20,256]{3,2,1,0:T(8,128)(2,1)}, bf16[16,1,20,256]{3,2,1,0:T(8,128)(2,1)}, u32[]{:S(2)}, u32[]{:S(2)}) collective-permute-start(bf16[16,1,20,256]{3,2,1,0:T(8,128)(2,1)} %get-tuple-element.78), channel_id=1, source_target_pairs={{1,0},{2,1},{3,2},{4,3},{5,4},{6,5},{7,6},{8,7},{9,8},{10,9},{11,1... | collective-permute-start | bytes 491528 | tf_op jit(solution)/shard_map/ppermute | solution.py:22
  759.7 13.9 %copy-start.26 = (bf16[16,2,18,255]{3,2,1,0:T(8,128)(2,1)S(1)}, bf16[16,2,18,255]{3,2,1,0:T(8,128)(2,1)}, u32[]{:S(2)}) copy-start(bf16[16,2,18,255]{3,2,1,0:T(8,128)(2,1)} %get-tuple-element.66) | copy-start | bytes 881284
  769.9 6.5 collective-permute-start.32
  773.5 3.7 collective-permute-start.33
  774.5 16.1 %copy-start.37 = (f32[3,3,1,16,16]{4,3,1,0,2:T(8,128)S(1)}, f32[3,3,1,16,16]{4,3,1,0,2:T(8,128)}, u32[]{:S(2)}) copy-start(f32[3,3,1,16,16]{4,3,1,0,2:T(8,128)} %convolution_bitcast_fusion.26) | copy-start | bytes 27652
  774.5 16.1 %copy-start.38 = (f32[3,3,1,16,16]{4,3,1,0,2:T(8,128)S(1)}, f32[3,3,1,16,16]{4,3,1,0,2:T(8,128)}, u32[]{:S(2)}) copy-start(f32[3,3,1,16,16]{4,3,1,0,2:T(8,128)} %convolution_bitcast_fusion.25) | copy-start | bytes 27652
  776.4 15.0 %copy-start.10 = (bf16[16,2,18,256]{3,2,1,0:T(8,128)(2,1)S(1)}, bf16[16,2,18,256]{3,2,1,0:T(8,128)(2,1)}, u32[]{:S(2)}) copy-start(bf16[16,2,18,256]{3,2,1,0:T(8,128)(2,1)} %copy-done.9) | copy-start | bytes 884740
  778.5 12.9 %collective-permute-start.34 = (bf16[16,1,20,256]{3,2,1,0:T(8,128)(2,1)S(1)}, bf16[16,1,20,256]{3,2,1,0:T(8,128)(2,1)S(1)}, u32[]{:S(2)}, u32[]{:S(2)}) collective-permute-start(bf16[16,1,20,256]{3,2,1,0:T(8,128)(2,1)S(1)} %get-tuple-element.73), channel_id=1, source_target_pairs={{0,1},{1,2},{2,3},{3,4},{4,5},{5,6},{6,7},{7,8},{8,9},{9,10},{10,1... | collective-permute-start | bytes 491528 | tf_op jit(solution)/shard_map/ppermute | solution.py:20
  778.6 12.8 %collective-permute-start.35 = (bf16[16,1,20,256]{3,2,1,0:T(8,128)(2,1)S(1)}, bf16[16,1,20,256]{3,2,1,0:T(8,128)(2,1)S(1)}, u32[]{:S(2)}, u32[]{:S(2)}) collective-permute-start(bf16[16,1,20,256]{3,2,1,0:T(8,128)(2,1)S(1)} %get-tuple-element.74), channel_id=1, source_target_pairs={{1,0},{2,1},{3,2},{4,3},{5,4},{6,5},{7,6},{8,7},{9,8},{10,9},{11,1... | collective-permute-start | bytes 491528 | tf_op jit(solution)/shard_map/ppermute | solution.py:22
  (54 other events, 258.2 us)
Sparse Core Ops, SparseCore 0:
  848.0 146.6 all-reduce.5
where the time goes:
time: 1020 us; the launch traced here: 1010 us
  local copies, waits for them, and re-layouts  519 us (51%)
  waiting for transfers between devices  178 us (17%)
  other arithmetic  124 us (12%)
  starting transfers between devices  94.2 us (9%)
  matrix products  77.3 us (8%)
  between operations  16 us (2%)
    psum x1, waiting for transfers between devices, local(): lax.psum((gradients[0], gradients[1], gradients[2], gradients[3]), ('grp'...  136 us
    another operation x7, local copies, waits for them, and re-layouts, filter_fields(): jnp.stack([velocity[left_comp] * velocity[right_comp] for left_comp, righ...  129 us
    unnamed x234, local copies, waits for them, and re-layouts  123 us
    ppermute x18, starting transfers between devices, with_halo(): lax.ppermute(head, axis, [((i + 1) % count, i) for i in range(count)])  64.2 us
    reshape x1, local copies, waits for them, and re-layouts, block_mean(): field.reshape(comps, cells_x // 2, 2, cells_y // 2, 2, cells_z // 2, 2)  58.8 us
    reduce_sum x2, other arithmetic, block_mean(): field.reshape(comps, cells_x // 2, 2, cells_y // 2, 2, cells_z // 2, 2)  52.2 us
    dot_general x12, matrix products, weight_gradient(): lax.dot_general(moved, columns, (((1,), (1,)), ((), ())), preferred_eleme...  42.5 us
    dot_general x21, matrix products, convolve(): jnp.dot(flat_kernel, columns, preferred_element_type=jnp.float32)  34.9 us
  transfers between devices with their start and end apart: 39, of which 10 were waited for; matrix products, arithmetic and copies ran while one was open for 23% of the time, Pallas kernels for 0%

commit v1 on v0

v1 whole, which is shorter than its diff:
```python
import jax
import jax.numpy as jnp
import numpy as np
from jax import lax
from jax.experimental import pallas as pl
from jax.experimental.pallas import tpu as pltpu
from jax.sharding import PartitionSpec as P

MESH = pl.DeviceIdType.MESH
F32 = jnp.float32
BF = jnp.bfloat16
GRP, SLAB = 4, 32
RY = 80
NB = 10
ROWS = NB * RY
OWN = 8 * RY
pair_table = ((0, 3, 4), (3, 1, 5), (4, 5, 2))
stress_pairs = ((0, 0), (1, 1), (2, 2), (0, 1), (0, 2), (1, 2))
SIZE = 6 * 64 * 72 * 256


def tables():
    fsel = np.zeros((256, 128), np.float32)
    for z in range(64):
        fsel[2 * z, z] = 1
        fsel[128 + 2 * z, 64 + z] = 1
    fedge = np.zeros((2, 384, 128), np.float32)
    fexp = np.zeros((256, NB * 128), np.float32)
    for f in range(3):
        for zi in range(8):
            fedge[0, f * 128 + 2 * (56 + zi), 64 + f * 8 + zi] = 1
            fedge[1, f * 128 + 2 * zi, 88 + f * 8 + zi] = 1
            fexp[192 + f * 8 + zi, zi * 16 + f] = 1
            fexp[216 + f * 8 + zi, 9 * 128 + zi * 16 + f] = 1
            for zb in range(8):
                fexp[f * 64 + zb * 8 + zi, (zb + 1) * 128 + zi * 16 + f] = 1
    texp = np.zeros((768, 1024), np.float32)
    comp = np.zeros((1024, 384), np.float32)
    cedge = np.zeros((2, 128, 128), np.float32)
    cexp = np.zeros((512, NB * 128), np.float32)
    for c in range(6):
        for zi in range(8):
            cedge[0, zi * 16 + c, c * 8 + zi] = 1
            cedge[1, zi * 16 + c, 48 + c * 8 + zi] = 1
            cexp[384 + c * 8 + zi, zi * 16 + c] = 1
            cexp[432 + c * 8 + zi, 9 * 128 + zi * 16 + c] = 1
            for zb in range(8):
                z = zb * 8 + zi
                texp[c * 128 + 2 * z, zb * 128 + zi * 16 + c] = 1
                comp[zb * 128 + zi * 16 + c, c * 64 + z] = 1
                cexp[c * 64 + z, (zb + 1) * 128 + zi * 16 + c] = 1
    vz = np.zeros((2, 1536, 128), np.float32)
    vze = np.zeros((128, 1536), np.float32)
    for p in range(12):
        for k in range(4):
            vz[0, p * 128 + 124 + k, p * 4 + k] = 1
            vz[1, p * 128 + k, 64 + p * 4 + k] = 1
            vze[p * 4 + k, p * 128 + 124 + k] = 1
            vze[64 + p * 4 + k, p * 128 + k] = 1
    pb = np.zeros((144, 160), np.float32)
    for y in range(144):
        at = y // 2
        pb[y, at] = 1
        for shift, value in ((-1, (-7, 1)), (0, (8, -8)), (1, (-1, 7))):
            if 0 <= at + shift < 72:
                pb[y, 80 + at + shift] = value[y % 2]

    def lane(c, z):
        if z < 0:
            return 384 + c * 8 + z + 8
        if z >= 64:
            return 432 + c * 8 + z - 64
        return c * 64 + z

    q1 = np.zeros((1024, 768), np.float32)
    q2 = np.zeros((512, 768), np.float32)
    for i in range(3):
        cx, cy, cz = pair_table[i]
        for z in range(-2, 130):
            out = i * 256 + (z if 0 <= z < 128 else (128 + z - 128 if z >= 128 else 256 + z))
            at = z // 2
            q1[lane(cx, at), out] = 1
            q2[lane(cy, at), out] = 1
            for shift, value in ((-1, (-7, 1)), (0, (8, -8)), (1, (-1, 7))):
                q1[512 + lane(cz, at + shift), out] = value[z % 2]
    spread = np.zeros((16, 128), np.float32)
    for zi in range(8):
        for c in range(16):
            spread[c, zi * 16 + c] = 1
    return [jnp.asarray(t, BF) for t in (fsel, fedge, fexp, texp, comp, cedge, cexp, vz, vze, pb, q1, q2, spread)]


def mm(a, b):
    return jnp.dot(a, b, preferred_element_type=F32)


def lanes(shape):
    return lax.broadcasted_iota(jnp.int32, shape, len(shape) - 1)


def write_plane(dst, p, value):
    low = lanes((ROWS, 128)) < 64
    dst[p, :, 0:128] = value.astype(BF)
    up = jnp.concatenate([value[RY:], value[:RY]], axis=0)
    down = jnp.concatenate([value[ROWS - RY :], value[: ROWS - RY]], axis=0)
    dst[p, :, 128:256] = jnp.where(low, up, down).astype(BF)


def conv_plane(src, p, kernel):
    lhs = jnp.concatenate([src[p], src[p + 1], src[p + 2]], axis=1)
    r = mm(lhs, kernel)
    return pltpu.roll(r[:, 0:128], 1, 0) + r[:, 128:256] + pltpu.roll(r[:, 256:384], ROWS - 1, 0)


def banded(w_ref, spread, wt):
    group = lanes((16, 128)) // 16

    @pl.loop(0, 7)
    def _(k):
        tile = mm(w_ref[k], spread)
        for dx in range(3):
            for dy in range(3):
                taps = [tile[(9 * dx + 3 * dy + dz) * 16 : (9 * dx + 3 * dy + dz + 1) * 16] for dz in range(3)]
                for slot in range(16):
                    z = -1 if slot == 15 else slot
                    value = jnp.zeros((16, 128), F32)
                    if slot <= 8 or slot == 15:
                        for dz in range(3):
                            value = jnp.where(group == z - (dz - 1), taps[dz], value)
                    wt[k, dx * 256 + slot * 16 : dx * 256 + slot * 16 + 16, dy * 128 : dy * 128 + 128] = value.astype(BF)


def weight_gradient(src, first, cots, gsrc, layer, gtmp):
    rhs = []
    for x in range(2):
        c = cots[x]
        rhs.append(jnp.concatenate([pltpu.roll(c, OWN - 1, 0), c, pltpu.roll(c, 1, 0)], axis=1).astype(BF))
    rhs = jnp.concatenate(rhs, axis=0)
    group = lanes((16, 128)) // 16
    for dx in range(3):
        lhs = jnp.concatenate([src[first + dx, RY : RY + OWN], src[first + dx + 1, RY : RY + OWN]], axis=0)
        gtmp[...] = lax.dot_general(lhs, rhs, (((0,), (0,)), ((), ())), preferred_element_type=F32)
        for dy in range(3):
            for dz in range(3):
                h = jnp.zeros((16, 128), F32)
                for zi in range(8):
                    z = zi + dz - 1
                    slot = 15 if z < 0 else z
                    h = h + jnp.where(group == zi, gtmp[slot * 16 : slot * 16 + 16, dy * 128 : dy * 128 + 128], 0.0)
                for step in (64, 32, 16):
                    h = h + pltpu.roll(h, step, 1)
                tap = 9 * dx + 3 * dy + dz
                old = gsrc[layer * 4 + tap // 8] if tap % 8 else jnp.zeros((16, 128), F32)
                gsrc[layer * 4 + tap // 8] = jnp.where(group == tap % 8, h, old)


def stencil(ref, p, t, r, count, low, force, scale):
    def at(i, dp, dy):
        return ref[i, p + dp, t, pl.ds(8 + r + dy, count), :]

    vel = [at(i, 0, 0) for i in range(3)]
    outs = []
    for i in range(3):
        f = vel[i]
        other = ref[i, p, 1 - t, pl.ds(8 + r, count), :]
        zp1 = pltpu.roll(jnp.where(low[0], other, f), 127, 1)
        zp2 = pltpu.roll(jnp.where(low[1], other, f), 126, 1)
        zm1 = pltpu.roll(jnp.where(low[2], other, f), 1, 1)
        zm2 = pltpu.roll(jnp.where(low[3], other, f), 2, 1)
        xp1, xp2, xm1, xm2 = at(i, 1, 0), at(i, 2, 0), at(i, -1, 0), at(i, -2, 0)
        yp1, yp2, ym1, ym2 = at(i, 0, 1), at(i, 0, 2), at(i, 0, -1), at(i, 0, -2)
        adv = vel[0] * (8.0 * (xp1 - xm1) - (xp2 - xm2))
        adv = adv + vel[1] * (8.0 * (yp1 - ym1) - (yp2 - ym2))
        adv = adv + vel[2] * (8.0 * (zp1 - zm1) - (zp2 - zm2))
        near = (xp1 + xm1) + (yp1 + ym1) + (zp1 + zm1)
        far = (xp2 + xm2) + (yp2 + ym2) + (zp2 + zm2)
        lap = 8.0 * near - 45.0 * f - 0.5 * far
        outs.append(scale * ((lap - adv) * (1.0 / 12.0) + force(i)))
    return vel, outs


def body(
    v, w7, fsel, fedge, fexp, texp, comp, cedge, cexp, vz, vze, pb, q1, q2, spread,
    vnext, sw, gout,
    fpx, fe, fer, vb, vbx, vzs, vzr, vzf, tx, wt, xe0, xe1, xe2, xe3, c4, xe4, xc3, xc2, xc1, mask,
    cpx, spx, ce, cer, se, ser, gxt, r2s, force, vext, fs, gtmp, gsrc, r1, r2g, ssem, rsem,
):
    g = lax.axis_index("grp")
    s = lax.axis_index("slab")
    used = [0]
    sent = []

    def slab_at(k):
        return {"slab": lax.rem(s + (k + SLAB), SLAB)}

    def grp_at(k):
        return {"grp": lax.rem(g + (k + GRP), GRP)}

    def send(src, dst, device):
        k = used[0]
        used[0] += 1
        copy = pltpu.make_async_remote_copy(
            src_ref=src, dst_ref=dst, send_sem=ssem.at[k], recv_sem=rsem.at[k], device_id=device, device_id_type=MESH
        )
        copy.start()
        sent.append(copy)
        return copy

    quad = lax.rem(s, 4)
    a = g * 4 + quad
    b = s // 4

    def peer_a(k):
        other = lax.rem(a + k, 16)
        return other, {"grp": other // 4, "slab": b * 4 + lax.rem(other, 4)}

    def peer_b(k):
        return {"slab": lax.rem(b + k, 8) * 4 + quad}

    barrier = pltpu.get_barrier_semaphore()
    friends = [slab_at(k) for k in (-3, -2, -1, 1, 2, 3)]
    friends += [peer_a(k)[1] for k in range(1, 16)] + [peer_b(k) for k in range(1, 8)]
    for friend in friends:
        pl.semaphore_signal(barrier, inc=1, device_id=friend, device_id_type=MESH)
    pl.semaphore_wait(barrier, len(friends))

    for X in range(2):
        fine = [[v[c, 2 * X + px, pl.ds(py, 72, stride=2), :] for px in range(2) for py in range(2)] for c in range(3)]

        def mean(parts):
            total = (parts[0] + parts[1]) + (parts[2] + parts[3])
            return (total + pltpu.roll(total, 127, 1)) * 0.125

        means = [mean(fine[c]) for c in range(3)]
        blank = jnp.zeros((8, 128), F32)
        fields = [jnp.concatenate([m, blank], axis=0).astype(BF) for m in means]
        targets = []
        for i, j in stress_pairs:
            t = mean([fine[i][n] * fine[j][n] for n in range(4)]) - means[i] * means[j]
            targets.append(jnp.concatenate([t, blank], axis=0).astype(BF))
        fpx[5 + X, :, 0:128] = mm(jnp.concatenate(fields[:2], axis=1), fsel[...]).astype(BF)
        fpx[5 + X, :, 128:256] = mm(fields[2], fsel[0:128]).astype(BF)
        joined = jnp.concatenate(fields, axis=1)
        for side in range(2):
            fe[side, X] = mm(joined, fedge[side]).astype(BF)
        t = mm(jnp.concatenate(targets, axis=1), texp[...])
        for zb in range(8):
            tx[X, zb * RY : zb * RY + RY] = t[:, zb * 128 : zb * 128 + 128]
    vb[...] = v[...].astype(BF)
    joined = jnp.concatenate([vb[c, x] for c in range(3) for x in range(4)], axis=1)
    for side in range(2):
        vzs[side] = mm(joined, vz[side]).astype(BF)

    zc = []
    for side, k in ((0, 1), (1, -1)):
        zc.append(send(fe.at[side], fer.at[side], grp_at(k)))
        zc.append(send(vzs.at[side], vzr.at[side], grp_at(k)))
    for copy in zc:
        copy.wait_recv()
    for X in range(2):
        fpx[5 + X, :, 128:256] = fpx[5 + X, :, 128:256] + fer[0, X] + fer[1, X]
    vzf[1] = vzr[0] + vzr[1]
    fc = []
    fc.append(send(fpx.at[pl.ds(5, 2)], fpx.at[pl.ds(3, 2)], slab_at(1)))
    fc.append(send(fpx.at[pl.ds(5, 2)], fpx.at[pl.ds(7, 2)], slab_at(-1)))
    fc.append(send(fpx.at[pl.ds(5, 2)], fpx.at[pl.ds(1, 2)], slab_at(2)))
    fc.append(send(fpx.at[pl.ds(5, 2)], fpx.at[pl.ds(9, 2)], slab_at(-2)))
    fc.append(send(fpx.at[pl.ds(6, 1)], fpx.at[pl.ds(0, 1)], slab_at(3)))
    fc.append(send(fpx.at[pl.ds(5, 1)], fpx.at[pl.ds(11, 1)], slab_at(-3)))
    vc = []
    for place, k in ((0, 1), (1, -1)):
        vc.append(send(vb, vbx.at[place], slab_at(k)))
        vc.append(send(vzf.at[1], vzf.at[2 * place], slab_at(k)))

    banded(w7, spread[...], wt)
    for zb in range(NB):
        mask[zb * RY : zb * RY + 72] = jnp.ones((72, 128), F32)
        mask[zb * RY + 72 : zb * RY + RY] = jnp.zeros((8, 128), F32)
    for copy in fc:
        copy.wait_recv()

    def expand(src, table, dst, count):
        @pl.loop(0, count)
        def _(p):
            r = mm(src[p], table[...])
            write_plane(dst, p, jnp.concatenate([r[:, zb * 128 : zb * 128 + 128] for zb in range(NB)], axis=0))

    expand(fpx, fexp, xe0, 12)

    for k, (src, dst, count) in enumerate(((xe0, xe1, 10), (xe1, xe2, 8), (xe2, xe3, 6))):

        @pl.loop(0, count)
        def _(p, src=src, dst=dst, k=k):
            write_plane(dst, p, jnp.tanh(conv_plane(src, p, wt[k])) * mask[...])

    for X in range(2):
        pred = (conv_plane(xe3, X + 1, wt[3]) * mask[...])[RY : RY + OWN]
        stress = pred.astype(BF)
        cot = (2.0 / SIZE * (pred - tx[X])).astype(BF)
        c4[X] = cot.astype(F32)
        for value, pack, edges, at in ((cot, cpx, ce, 3), (stress, spx, se, 2)):
            joined = jnp.concatenate([value[zb * RY : zb * RY + RY] for zb in range(8)], axis=1)
            pack[at + X, :, 0:384] = mm(joined, comp[...]).astype(BF)
            edges[0, X] = mm(value[7 * RY : 8 * RY], cedge[0]).astype(BF)
            edges[1, X] = mm(value[0:RY], cedge[1]).astype(BF)

    zc = []
    for side, k in ((0, 1), (1, -1)):
        zc.append(send(ce.at[side], cer.at[side], grp_at(k)))
        zc.append(send(se.at[side], ser.at[side], grp_at(k)))
    for copy in zc:
        copy.wait_recv()
    for X in range(2):
        cpx[3 + X, :, 384:512] = cer[0, X] + cer[1, X]
        spx[2 + X, :, 384:512] = ser[0, X] + ser[1, X]
    cc = []
    cc.append(send(cpx.at[pl.ds(3, 2)], cpx.at[pl.ds(1, 2)], slab_at(1)))
    cc.append(send(cpx.at[pl.ds(3, 2)], cpx.at[pl.ds(5, 2)], slab_at(-1)))
    cc.append(send(cpx.at[pl.ds(4, 1)], cpx.at[pl.ds(0, 1)], slab_at(2)))
    cc.append(send(cpx.at[pl.ds(3, 1)], cpx.at[pl.ds(7, 1)], slab_at(-2)))
    sc = []
    sc.append(send(spx.at[pl.ds(2, 2)], spx.at[pl.ds(0, 2)], slab_at(1)))
    sc.append(send(spx.at[pl.ds(2, 2)], spx.at[pl.ds(4, 2)], slab_at(-1)))
    wc = []
    for k in range(1, GRP):
        other = lax.rem(g + k, GRP)
        rows = pl.ds(pl.multiple_of(other * 16, 16), 32)
        wc.append(send(spx.at[pl.ds(2, 2), rows, pl.ds(0, 384)], sw.at[g], grp_at(k)))
    rows = pl.ds(pl.multiple_of(g * 16, 16), 32)
    sw[g] = spx[2:4, rows, 0:384]

    weight_gradient(xe3, 1, [c4[0], c4[1]], gsrc, 3, gtmp)

    for copy in vc:
        copy.wait_recv()
    pads = jnp.zeros((8, 128), F32)
    for c in range(3):

        @pl.loop(0, 12)
        def _(p, c=c):
            for t in range(2):
                vext[c, p, t, 0:8] = pads
                vext[c, p, t, 152:160] = pads

        @pl.loop(0, 8)
        def _(p, c=c):
            for t in range(2):
                fs[c, p, t, 0:8] = pads
                fs[c, p, t, 152:160] = pads

        for x in range(4):
            vext[c, x, 0, 8:152] = vbx[0, c, x].astype(F32)
            vext[c, 4 + x, 0, 8:152] = v[c, x]
            vext[c, 8 + x, 0, 8:152] = vbx[1, c, x].astype(F32)
    for n in range(3):
        r = mm(vzf[n], vze[...])
        for c in range(3):
            for x in range(4):
                p = c * 4 + x
                vext[c, 4 * n + x, 1, 8:152] = r[:, p * 128 : p * 128 + 128]

    for copy in cc:
        copy.wait_recv()
    expand(cpx, cexp, xe4, 8)

    def back(src, k, act, shift, dst, count):
        @pl.loop(0, count)
        def _(p):
            below = act[p + shift, :, 0:128].astype(F32)
            write_plane(dst, p, conv_plane(src, p, wt[k]) * (1.0 - below * below) * mask[...])

    def own(ref, at):
        return [ref[at + X, RY : RY + OWN, 0:128].astype(F32) for X in range(2)]

    back(xe4, 4, xe3, 0, xc3, 6)
    weight_gradient(xe2, 2, own(xc3, 2), gsrc, 2, gtmp)
    back(xc3, 5, xe2, 2, xc2, 4)
    weight_gradient(xe1, 3, own(xc2, 1), gsrc, 1, gtmp)
    back(xc2, 6, xe1, 4, xc1, 2)
    weight_gradient(xe0, 4, own(xc1, 0), gsrc, 0, gtmp)

    first = [send(gsrc.at[peer_a(k)[0]], r1.at[k - 1], peer_a(k)[1]) for k in range(1, 16)]

    for copy in sc:
        copy.wait_recv()
    for n in range(8):
        at = 1 + n // 2
        lower, mid, upper = (spx[at + d].astype(F32) for d in (-1, 0, 1))
        if n % 2 == 0:
            slope = 8.0 * mid - upper - 7.0 * lower
        else:
            slope = 7.0 * upper - 8.0 * mid + lower
        gxt[n * RY : n * RY + RY, 0:512] = slope.astype(BF)
        gxt[n * RY : n * RY + RY, 512:1024] = spx[at]
        if n % 2 == 0:
            r2s[n // 2] = mm(spx[at], q2[...]).astype(BF)
    r = mm(gxt[...], q1[...]).astype(BF)
    for n in range(8):
        both = jnp.concatenate([r[n * RY : n * RY + RY], r2s[n // 2]], axis=0)
        force[n] = mm(pb[...], both) * (-4.0 / 12.0)

    for copy in first:
        copy.wait_recv()
    total = gsrc[a]
    for k in range(15):
        total = total + r1[k]
    r2g[b] = total
    second = [send(r2g.at[b], r2g.at[b], peer_b(k)) for k in range(1, 8)]

    count = 48
    lane = lanes((count, 128))
    low = (lane < 1, lane < 2, lane >= 127, lane >= 126)

    @pl.loop(0, 8)
    def _(p):
        for t in range(2):
            for r in range(0, 144, count):
                vel, outs = stencil(
                    vext, p + 2, t, r, count, low,
                    lambda i: force[p, r : r + count, i * 256 + t * 128 : i * 256 + t * 128 + 128], 0.1,
                )
                for i in range(3):
                    fs[i, p, t, 8 + r : 8 + r + count] = vel[i] + outs[i]

    for copy in second:
        copy.wait_recv()
    total = r2g[0]
    for k in range(1, 8):
        total = total + r2g[k]
    gout[a] = total
    third = [send(gout.at[a], gout.at[a], peer_a(k)[1]) for k in range(1, 16)]

    @pl.loop(0, 4)
    def _(x):
        for r in range(0, 144, count):
            vel, outs = stencil(
                fs, x + 2, 0, r, count, low,
                lambda i: force[x + 2, r : r + count, i * 256 : i * 256 + 128], 0.1,
            )
            for i in range(3):
                vnext[i, x, r : r + count] = 0.5 * (v[i, x, r : r + count] + vel[i] + outs[i])

    for copy in third:
        copy.wait_recv()
    for copy in wc:
        copy.wait_recv()
    for copy in sent:
        copy.wait_send()


def forward_rows(weight):
    padded = jnp.pad(weight, ((0, 0), (0, 16 - weight.shape[1]), (0, 16 - weight.shape[2])))
    return jnp.transpose(padded, (0, 2, 1)).reshape(432, 16)


def backward_rows(weight):
    padded = jnp.pad(weight, ((0, 0), (0, 16 - weight.shape[1]), (0, 16 - weight.shape[2])))
    return padded[::-1].reshape(432, 16)


def local(velocity, w_in, w_mid_a, w_mid_b, w_out):
    w7 = jnp.stack(
        [forward_rows(w) for w in (w_in, w_mid_a, w_mid_b, w_out)]
        + [backward_rows(w) for w in (w_out, w_mid_b, w_mid_a)]
    )
    vm = pltpu.VMEM
    scratch = [
        vm((12, RY, 256), BF), vm((2, 2, RY, 128), BF), vm((2, 2, RY, 128), BF),
        vm((3, 4, 144, 128), BF), vm((2, 3, 4, 144, 128), BF),
        vm((2, 144, 128), BF), vm((2, 144, 128), BF), vm((3, 144, 128), BF),
        vm((2, OWN, 128), F32), vm((7, 768, 384), BF),
        vm((12, ROWS, 256), BF), vm((10, ROWS, 256), BF), vm((8, ROWS, 256), BF), vm((6, ROWS, 256), BF),
        vm((2, OWN, 128), F32),
        vm((8, ROWS, 256), BF), vm((6, ROWS, 256), BF), vm((4, ROWS, 256), BF), vm((2, ROWS, 256), BF),
        vm((ROWS, 128), F32),
        vm((8, RY, 512), BF), vm((6, RY, 512), BF),
        vm((2, 2, RY, 128), BF), vm((2, 2, RY, 128), BF), vm((2, 2, RY, 128), BF), vm((2, 2, RY, 128), BF),
        vm((8 * RY, 1024), BF), vm((4, RY, 768), BF), vm((8, 144, 768), F32),
        vm((3, 12, 2, 160, 128), F32), vm((3, 8, 2, 160, 128), F32),
        vm((256, 384), F32), vm((16, 16, 128), F32), vm((15, 16, 128), F32), vm((8, 16, 128), F32),
        pltpu.SemaphoreType.DMA((64,)), pltpu.SemaphoreType.DMA((64,)),
    ]
    consts = tables()
    vnext, sw, gout = pl.pallas_call(
        body,
        out_shape=[
            jax.ShapeDtypeStruct((3, 4, 144, 128), F32),
            jax.ShapeDtypeStruct((4, 2, 32, 384), BF),
            jax.ShapeDtypeStruct((16, 16, 128), F32),
        ],
        in_specs=[pl.BlockSpec(memory_space=pltpu.VMEM)] * (2 + len(consts)),
        out_specs=[pl.BlockSpec(memory_space=pltpu.VMEM)] * 3,
        scratch_shapes=scratch,
        compiler_params=pltpu.CompilerParams(
            collective_id=0, has_side_effects=True, vmem_limit_bytes=62 * 1024 * 1024
        ),
    )(velocity, w7, *consts)
    g = lax.axis_index("grp")
    window = lax.dynamic_slice_in_dim(sw, 2 * g, 18, axis=2).reshape(4, 2, 18, 6, 64)
    stress = jnp.transpose(window, (3, 1, 2, 0, 4)).reshape(6, 2, 18, 256)
    grads = jnp.transpose(gout.reshape(4, 4, 16, 8, 16), (0, 1, 3, 4, 2)).reshape(4, 32, 16, 16)
    return (
        vnext, stress,
        grads[0, :27, :, :3], grads[1, :27], grads[2, :27], grads[3, :27, :6],
    )


def solution(mesh):
    in_specs = (P(None, "slab", None, "grp"), P(), P(), P(), P())
    out_specs = (P(None, "slab", None, "grp"), P(None, "slab", "grp", None), P(), P(), P(), P())
    return jax.shard_map(local, mesh=mesh, in_specs=in_specs, out_specs=out_specs, check_vma=False)
```

time: 1020 us -> 126 us (0.12); the launches traced: 1010 us -> 126 us
  local copies, waits for them, and re-layouts: 519 us -> 14.1 us
  waiting for transfers between devices: 178 us -> 0 us
  other arithmetic: 124 us -> 0 us
  Pallas kernels: 0 us -> 111 us
  starting transfers between devices: 94.2 us -> 0 us
  matrix products: 77.3 us -> 0 us
  between operations: 16 us -> 0.81 us
    reshape x59 -> x3, local copies, waits for them, and re-layouts: 161 us -> 1.39 us  [the longest x1 0.85 us: local(): stress = jnp.transpose(window, (3, 1, 2, 0, 4)).reshape(6, 2, 18, 256)]
    psum x1 -> x0, waiting for transfers between devices: 136 us -> none  [local(): lax.psum((gradients[0], gradients[1], gradients[2], gradients[3]), ('grp'...]
    another operation x19 -> x9, local copies, waits for them, and re-layouts: 136 us -> 2.41 us  [local(): jnp.stack([forward_rows(w) for w in (w_in, w_mid_a, w_mid_b, w_out)] + [b...]
    unnamed x234 -> x18, local copies, waits for them, and re-layouts: 123 us -> 3.36 us
    pallas_call x0 -> x1, Pallas kernels: none -> 111 us  [local(): pl.pallas_call(body, out_shape=[jax.ShapeDtypeStruct((3, 4, 144, 128), F3...]
    ppermute x36 -> x0, starting transfers between devices: 85.1 us -> none  [the longest x18 64.2 us: with_halo(): lax.ppermute(head, axis, [((i + 1) % count, i) for i in range(count)])]
    dot_general x33 -> x0, matrix products: 77.3 us -> none  [the longest x12 42.5 us: weight_gradient(): lax.dot_general(moved, columns, (((1,), (1,)), ((), ())), preferred_eleme...]
    slice x56 -> x2, local copies, waits for them, and re-layouts: 55.8 us -> 0.83 us  [local(): grads[0, :27, :, :3]]
  transfers between devices with their start and end apart: 39 -> 0, of which waited for: 10 -> 0; matrix products, arithmetic and copies ran while one was open for 23% -> 0% of each run, Pallas kernels for 0% -> 0%
where the time goes in v1:
time: 126 us
  Pallas kernels  111 us (88%)
  local copies, waits for them, and re-layouts  14.1 us (11%)
    pallas_call x1, Pallas kernels, local(): pl.pallas_call(body, out_shape=[jax.ShapeDtypeStruct((3, 4, 144, 128), F3...  111 us
    unnamed x18, local copies, waits for them, and re-layouts  3.36 us
    transpose x5, local copies, waits for them, and re-layouts, forward_rows(): return jnp.transpose(padded, (0, 2, 1)).reshape(432, 16)  3.15 us

profile of v1, /device:TPU:1, one launch (start us, length us, event | category | flops | bytes accessed | tf_op | source)
XLA Modules:
  0.0 125.7 jit_solution(1851913113263295687)
XLA Ops:
  0.6 0.0 copy-start.2
  0.6 0.0 copy-start.1
  0.7 0.8 fusion
  1.5 0.2 copy.77
  1.7 0.2 stack_reshape.24
  1.8 0.7 pad_bitcast_fusion
  2.6 0.2 copy.74
  2.8 0.2 stack_reshape.21
  2.9 1.0 copy.75
  4.0 0.2 stack_reshape.22
  4.2 1.0 copy.76
  5.2 0.2 stack_reshape.23
  5.4 0.1 rev.9
  5.5 0.2 copy.78
  5.7 0.2 stack_reshape.25
  5.9 0.0 copy-done.1
  5.9 0.1 rev.10
  6.0 0.2 copy.79
  6.2 0.2 stack_reshape.26
  6.4 0.0 copy-done.2
  6.4 0.1 rev.11
  6.5 0.2 copy.80
  6.7 0.2 stack_reshape.27
  6.9 1.2 copy.81.w7
  8.0 110.8 %shard_map.217 = (f32[3,4,144,128]{3,2,1,0:T(8,128)}, bf16[4,2,32,384]{3,2,1,0:T(8,128)(2,1)}, f32[16,16,128]{2,1,0:T(8,128)}) custom-call(f32[3,4,144,128]{3,2,1,0:T(8,128)} %v.1, bf16[7,432,16]{2,1,0:T(8,128)(2,1)} %copy.81.w7, bf16[256,128]{1,0:T(8,128)(2,1)} %constant.40.clone.fsel, bf16[2,384,128]{2,1,0:T(8,128)(2,1)} %constant.41.clone.fedge, ...), custom_call_target="tpu_custom_call" | custom-call | tf_op jit(solution)/shard_map/pallas_call | solution.py:484
  118.8 0.0 copy-start.3
  118.8 1.0 constant_dynamic-slice_fusion
  119.8 0.1 copy.82
  119.9 0.2 reshape.24
  120.2 0.1 copy.83
  120.3 0.8 reshape.25
  121.1 0.0 copy-done.3
  121.1 0.3 copy.89
  121.5 0.0 copy-start
  121.5 0.8 copy.86
  122.4 0.8 copy.87
  123.2 0.8 copy.85
  124.0 0.7 copy.88
  124.8 0.0 copy-done
  124.8 0.9 copy.97
  (10 shorter events, 0.1 us)
Async XLA Ops:
  0.6 5.7 %copy-start.2 = (bf16[27,16,16]{0,2,1:T(8,128)(2,1)S(1)}, bf16[27,16,16]{0,2,1:T(8,128)(2,1)}, u32[]{:S(2)}) copy-start(bf16[27,16,16]{0,2,1:T(8,128)(2,1)} %param.20) | copy-start | bytes 41476
  0.6 5.2 %copy-start.1 = (bf16[27,16,16]{0,2,1:T(8,128)(2,1)S(1)}, bf16[27,16,16]{0,2,1:T(8,128)(2,1)}, u32[]{:S(2)}) copy-start(bf16[27,16,16]{0,2,1:T(8,128)(2,1)} %param.21) | copy-start | bytes 41476
  118.8 2.3 %copy-start.3 = (f32[16,16,128]{2,1,0:T(8,128)S(1)}, f32[16,16,128]{2,1,0:T(8,128)}, u32[]{:S(2)}) copy-start(f32[16,16,128]{2,1,0:T(8,128)} %get-tuple-element.11) | copy-start | bytes 393220
  121.5 3.3 %copy-start = (f32[3,4,144,128]{3,2,1,0:T(8,128)S(1)}, f32[3,4,144,128]{3,2,1,0:T(8,128)}, u32[]{:S(2)}) copy-start(f32[3,4,144,128]{3,2,1,0:T(8,128)} %get-tuple-element.46) | copy-start | bytes 2654212

commit v2 on v1

v2 whole, which is shorter than its diff:
```python
import jax
import jax.numpy as jnp
import numpy as np
from jax import lax
from jax.experimental import pallas as pl
from jax.experimental.pallas import tpu as pltpu
from jax.sharding import PartitionSpec as P

MESH = pl.DeviceIdType.MESH
F32 = jnp.float32
BF = jnp.bfloat16
GRP, SLAB = 4, 32
RY = 80
NB = 10
ROWS = NB * RY
OWN = 8 * RY
pair_table = ((0, 3, 4), (3, 1, 5), (4, 5, 2))
stress_pairs = ((0, 0), (1, 1), (2, 2), (0, 1), (0, 2), (1, 2))
SIZE = 6 * 64 * 72 * 256


def tables():
    fsel = np.zeros((256, 128), np.float32)
    for z in range(64):
        fsel[2 * z, z] = 1
        fsel[128 + 2 * z, 64 + z] = 1
    fedge = np.zeros((2, 384, 128), np.float32)
    fexp = np.zeros((256, NB * 128), np.float32)
    for f in range(3):
        for zi in range(8):
            fedge[0, f * 128 + 2 * (56 + zi), 64 + f * 8 + zi] = 1
            fedge[1, f * 128 + 2 * zi, 88 + f * 8 + zi] = 1
        for block in range(NB):
            for kz in range(10):
                z = block * 8 - 9 + kz
                if -8 <= z < 72:
                    at = f * 64 + z if 0 <= z < 64 else (200 + f * 8 + z if z < 0 else 152 + f * 8 + z)
                    fexp[at, block * 128 + kz * 4 + f] = 1
    texp = np.zeros((768, 1024), np.float32)
    comp = np.zeros((1024, 384), np.float32)
    cedge = np.zeros((2, 128, 128), np.float32)
    cexp = np.zeros((512, NB * 128), np.float32)
    for c in range(6):
        for zi in range(8):
            cedge[0, zi * 16 + c, c * 8 + zi] = 1
            cedge[1, zi * 16 + c, 48 + c * 8 + zi] = 1
            for zb in range(8):
                z = zb * 8 + zi
                texp[c * 128 + 2 * z, zb * 128 + zi * 16 + c] = 1
                comp[zb * 128 + zi * 16 + c, c * 64 + z] = 1
        for block in range(NB):
            for kz in range(10):
                z = block * 8 - 9 + kz
                if -8 <= z < 72:
                    at = c * 64 + z if 0 <= z < 64 else (392 + c * 8 + z if z < 0 else 368 + c * 8 + z)
                    cexp[at, block * 128 + kz * 6 + c] = 1
    vz = np.zeros((2, 1536, 128), np.float32)
    vze = np.zeros((128, 1536), np.float32)
    for p in range(12):
        for k in range(4):
            vz[0, p * 128 + 124 + k, p * 4 + k] = 1
            vz[1, p * 128 + k, 64 + p * 4 + k] = 1
            vze[p * 4 + k, p * 128 + 124 + k] = 1
            vze[64 + p * 4 + k, p * 128 + k] = 1
    pb = np.zeros((144, 160), np.float32)
    for y in range(144):
        at = y // 2
        pb[y, at] = 1
        for shift, value in ((-1, (-7, 1)), (0, (8, -8)), (1, (-1, 7))):
            if 0 <= at + shift < 72:
                pb[y, 80 + at + shift] = value[y % 2]

    def lane(c, z):
        if z < 0:
            return 384 + c * 8 + z + 8
        if z >= 64:
            return 432 + c * 8 + z - 64
        return c * 64 + z

    q1 = np.zeros((1024, 768), np.float32)
    q2 = np.zeros((512, 768), np.float32)
    for i in range(3):
        cx, cy, cz = pair_table[i]
        for z in range(-2, 130):
            out = i * 256 + (z if 0 <= z < 128 else (128 + z - 128 if z >= 128 else 256 + z))
            at = z // 2
            q1[lane(cx, at), out] = 1
            q2[lane(cy, at), out] = 1
            for shift, value in ((-1, (-7, 1)), (0, (8, -8)), (1, (-1, 7))):
                q1[512 + lane(cz, at + shift), out] = value[z % 2]
    spread = np.zeros((16, 128), np.float32)
    for zi in range(8):
        for c in range(16):
            spread[c, zi * 16 + c] = 1
    return [jnp.asarray(t, BF) for t in (fsel, fedge, fexp, texp, comp, cedge, cexp, vz, vze, pb, q1, q2, spread)]


def mm(a, b):
    return jnp.dot(a, b, preferred_element_type=F32)


def lanes(shape):
    return lax.broadcasted_iota(jnp.int32, shape, len(shape) - 1)


def edge_group(dx, z):
    return (7, 1, 3)[dx] if z < 0 else (0, 2, 4)[dx]


def row_of(dx, z):
    return dx * 128 + z * 16 if 0 <= z < 8 else 384 + edge_group(dx, z) * 16


def write_plane(dst, p, value):
    lane = lanes((ROWS, 128))
    dst[p, :, 0:128] = value.astype(BF)
    up = jnp.concatenate([value[RY:], value[:RY]], axis=0)
    down = jnp.concatenate([value[ROWS - RY :], value[: ROWS - RY]], axis=0)
    edge = jnp.where(lane < 16, up, jnp.where(lane >= 112, down, 0.0))
    dst[p, :, 128:256] = edge.astype(BF)
    dst[p, :, 256:384] = pltpu.roll(edge, 32, 1).astype(BF)
    dst[p, :, 384:512] = pltpu.roll(edge, 64, 1).astype(BF)


def window(src, p, rows):
    edges = src[p, rows, 128:256] + src[p + 1, rows, 256:384] + src[p + 2, rows, 384:512]
    return jnp.concatenate([src[p, rows, 0:128], src[p + 1, rows, 0:128], src[p + 2, rows, 0:128], edges], axis=1)


def window_fields(src, p, rows):
    return src[p, rows, 0:128] + src[p + 1, rows, 128:256] + src[p + 2, rows, 256:384]


def window_cot(src, p, rows):
    low, mid, high = (lax.rem(p + 8 + k, 12) for k in range(3))
    return jnp.concatenate([src[low, rows, 0:128] + src[mid, rows, 128:256], src[high, rows, 0:128]], axis=1)


def conv_plane(lhs, kernel):
    r = mm(lhs, kernel)
    return pltpu.roll(r[:, 0:128], 1, 0) + r[:, 128:256] + pltpu.roll(r[:, 256:384], ROWS - 1, 0)


ALL = slice(0, ROWS)
MID = slice(RY, RY + OWN)


def banded(w_in, w_a, w_b, w_out, spread, wt, w1, w4, wf, tiles):
    group = lanes((16, 128)) // 16

    def turned(w, tap):
        return lax.dot_general(w[tap], spread[0 : w.shape[1]], (((0,), (0,)), ((), ())), preferred_element_type=F32)

    def fill(out):
        for dx in range(3):
            for dy in range(3):
                at = slice(dy * 128, dy * 128 + 128)
                for z in range(-1, 9):
                    value = jnp.zeros((16, 128), F32)
                    for dz in range(3):
                        value = jnp.where(group == z - (dz - 1), tiles[9 * dx + 3 * dy + dz], value)
                    row = row_of(dx, z)
                    wt[out, row : row + 16, at] = value.astype(BF)
        wt[out, 464:496] = jnp.zeros((32, 384), BF)

    for out, w in enumerate((w_a, w_b, w_out)):
        for tap in range(27):
            tiles[tap] = turned(w, tap)
        fill(out)
    for out, w in ((3, w_b), (4, w_a)):
        for tap in range(27):
            tiles[tap] = mm(w[26 - tap], spread)
        fill(out)

    def small(count, starts):
        wf[...] = jnp.zeros((256, 384), F32)
        part = lanes((count, 128)) // 16
        for dx in range(3):
            for dy in range(3):
                for kz in range(10):
                    value = jnp.zeros((count, 128), F32)
                    for dz in range(3):
                        value = jnp.where(part == kz - dz, tiles[9 * dx + 3 * dy + dz, 0:count], value)
                    row = starts[dx] + kz * count
                    wf[row : row + count, dy * 128 : dy * 128 + 128] = value

    for tap in range(27):
        tiles[tap, 0:3] = turned(w_in, tap)
        tiles[tap, 3:4] = jnp.zeros((1, 128), F32)
    small(4, (0, 40, 80))
    w1[...] = wf[0:128].astype(BF)
    for tap in range(27):
        tiles[tap, 0:6] = mm(w_out[26 - tap], spread)
    small(6, (0, 60, 128))
    w4[...] = wf[...].astype(BF)


def shifted_cots(cots):
    both = [
        jnp.concatenate([pltpu.roll(c, OWN - 1, 0), c, pltpu.roll(c, 1, 0)], axis=1).astype(BF) for c in cots
    ]
    return jnp.concatenate(both, axis=0)


def keep_tap(gsrc, layer, tap, h):
    group = lanes((16, 128)) // 16
    old = gsrc[layer * 4 + tap // 8] if tap % 8 else jnp.zeros((16, 128), F32)
    gsrc[layer * 4 + tap // 8] = jnp.where(group == tap % 8, h, old)


def weight_gradient(src, first, cots, gsrc, layer, gtmp):
    rhs = jnp.concatenate([window(src, first + x, MID) for x in range(2)], axis=0)
    gtmp[...] = lax.dot_general(shifted_cots(cots), rhs, (((0,), (0,)), ((), ())), preferred_element_type=F32)
    group = lanes((16, 128)) // 16
    for dx in range(3):
        for dy in range(3):
            for dz in range(3):
                h = jnp.zeros((16, 128), F32)
                extra = None
                for zi in range(8):
                    z = zi + dz - 1
                    row = slice(dy * 128 + zi * 16, dy * 128 + zi * 16 + 16)
                    if 0 <= z < 8:
                        h = jnp.where(group == z, gtmp[row, dx * 128 : dx * 128 + 128], h)
                    else:
                        extra = jnp.where(group == edge_group(dx, z), gtmp[row, 384:512], 0.0)
                if extra is not None:
                    h = h + extra
                for step in (64, 32, 16):
                    h = h + pltpu.roll(h, step, 1)
                keep_tap(gsrc, layer, 9 * dx + 3 * dy + dz, h)


def first_gradient(src, first, cots, gsrc, gtmp):
    rhs = jnp.concatenate([window_fields(src, first + x, MID) for x in range(2)], axis=0)
    gtmp[:, 0:128] = lax.dot_general(shifted_cots(cots), rhs, (((0,), (0,)), ((), ())), preferred_element_type=F32)
    part = lanes((16, 128)) // 4
    for dx in range(3):
        for dy in range(3):
            for dz in range(3):
                h = jnp.zeros((16, 128), F32)
                for zi in range(8):
                    row = slice(dy * 128 + zi * 16, dy * 128 + zi * 16 + 16)
                    h = jnp.where(part == dx * 10 + zi + dz, gtmp[row, 0:128], h)
                for step in (112, 120, 124):
                    h = h + pltpu.roll(h, step, 1)
                tap = 9 * dx + 3 * dy + dz
                turn = ((tap % 8) * 16 - (dx * 40 + dz * 4)) % 128
                keep_tap(gsrc, 0, tap, pltpu.roll(h, turn, 1) if turn else h)


def stencil(ref, p, t, r, count, low):
    def at(i, dp, dy):
        return ref[i, p + dp, t, pl.ds(8 + r + dy, count), :]

    vel = [at(i, 0, 0) for i in range(3)]
    outs = []
    for i in range(3):
        f = vel[i]
        other = ref[i, p, 1 - t, pl.ds(8 + r, count), :]
        zp1 = pltpu.roll(jnp.where(low[0], other, f), 127, 1)
        zp2 = pltpu.roll(jnp.where(low[1], other, f), 126, 1)
        zm1 = pltpu.roll(jnp.where(low[2], other, f), 1, 1)
        zm2 = pltpu.roll(jnp.where(low[3], other, f), 2, 1)
        xp1, xp2, xm1, xm2 = at(i, 1, 0), at(i, 2, 0), at(i, -1, 0), at(i, -2, 0)
        yp1, yp2, ym1, ym2 = at(i, 0, 1), at(i, 0, 2), at(i, 0, -1), at(i, 0, -2)
        adv = vel[0] * (8.0 * (xp1 - xm1) - (xp2 - xm2))
        adv = adv + vel[1] * (8.0 * (yp1 - ym1) - (yp2 - ym2))
        adv = adv + vel[2] * (8.0 * (zp1 - zm1) - (zp2 - zm2))
        near = (xp1 + xm1) + (yp1 + ym1) + (zp1 + zm1)
        far = (xp2 + xm2) + (yp2 + ym2) + (zp2 + zm2)
        lap = 8.0 * near - 45.0 * f - 0.5 * far
        outs.append((lap - adv) * (0.1 / 12.0))
    return vel, outs


def body(
    v, w_in, w_a, w_b, w_out, spread, *refs
):
    far = refs[:12]
    vnext, sw, gout = refs[12:15]
    near = refs[15:27]
    fsel, fedge, fexp, texp, comp, cedge, cexp, vz, vze, pb, q1, q2 = near
    (
        fpx, fe, fer, vb, vbx, vzs, vzr, vzf, tx, wt, w1, w4, wf, tiles, xe0, xe1, xe2, xe3, c4, c1, mask,
        cpx, spx, ce, cer, se, ser, gxt, r2s, force, vext, fs, gtmp, gsrc, r1, r2g, csem, ssem, rsem,
    ) = refs[27:]
    held = [pltpu.make_async_copy(far[n], near[n], csem.at[n]) for n in range(12)]
    for copy in held:
        copy.start()
    g = lax.axis_index("grp")
    s = lax.axis_index("slab")
    used = [0]
    sent = []

    def slab_at(k):
        return {"slab": lax.rem(s + (k + SLAB), SLAB)}

    def grp_at(k):
        return {"grp": lax.rem(g + (k + GRP), GRP)}

    def send(src, dst, device):
        k = used[0]
        used[0] += 1
        copy = pltpu.make_async_remote_copy(
            src_ref=src, dst_ref=dst, send_sem=ssem.at[k], recv_sem=rsem.at[k], device_id=device, device_id_type=MESH
        )
        copy.start()
        sent.append(copy)
        return copy

    quad = lax.rem(s, 4)
    a = g * 4 + quad
    b = s // 4

    def peer_a(k):
        other = lax.rem(a + k, 16)
        return other, {"grp": other // 4, "slab": b * 4 + lax.rem(other, 4)}

    def peer_b(k):
        return {"slab": lax.rem(b + k, 8) * 4 + quad}

    barrier = pltpu.get_barrier_semaphore()
    friends = [slab_at(k) for k in (-3, -2, -1, 1, 2, 3)]
    friends += [peer_a(k)[1] for k in range(1, 16)] + [peer_b(k) for k in range(1, 8)]
    for friend in friends:
        pl.semaphore_signal(barrier, inc=1, device_id=friend, device_id_type=MESH)

    held[0].wait()
    held[1].wait()
    parts = []
    blank = jnp.zeros((8, 128), F32)

    def mean(four):
        total = (four[0] + four[1]) + (four[2] + four[3])
        return (total + pltpu.roll(total, 127, 1)) * 0.125

    for X in range(2):
        fine = [[v[c, 2 * X + px, pl.ds(py, 72, stride=2), :] for px in range(2) for py in range(2)] for c in range(3)]
        means = [mean(fine[c]) for c in range(3)]
        parts.append((fine, means))
        fields = [jnp.concatenate([m, blank], axis=0).astype(BF) for m in means]
        fpx[5 + X, :, 0:128] = mm(jnp.concatenate(fields[:2], axis=1), fsel[...]).astype(BF)
        fpx[5 + X, :, 128:256] = mm(fields[2], fsel[0:128]).astype(BF)
        joined = jnp.concatenate(fields, axis=1)
        for side in range(2):
            fe[side, X] = mm(joined, fedge[side]).astype(BF)
    pl.semaphore_wait(barrier, len(friends))
    zc = [send(fe.at[side], fer.at[side], grp_at(k)) for side, k in ((0, 1), (1, -1))]

    vb[...] = v[...].astype(BF)
    held[7].wait()
    joined = jnp.concatenate([vb[c, x] for c in range(3) for x in range(4)], axis=1)
    for side in range(2):
        vzs[side] = mm(joined, vz[side]).astype(BF)
    uc = [send(vzs.at[side], vzr.at[side], grp_at(k)) for side, k in ((0, 1), (1, -1))]

    for copy in zc:
        copy.wait_recv()
    for X in range(2):
        fpx[5 + X, :, 128:256] = fpx[5 + X, :, 128:256] + fer[0, X] + fer[1, X]
    fc = []
    fc.append(send(fpx.at[pl.ds(5, 2)], fpx.at[pl.ds(3, 2)], slab_at(1)))
    fc.append(send(fpx.at[pl.ds(5, 2)], fpx.at[pl.ds(7, 2)], slab_at(-1)))
    fc.append(send(fpx.at[pl.ds(6, 1)], fpx.at[pl.ds(0, 1)], slab_at(3)))
    fc.append(send(fpx.at[pl.ds(5, 1)], fpx.at[pl.ds(11, 1)], slab_at(-3)))
    fc.append(send(fpx.at[pl.ds(5, 2)], fpx.at[pl.ds(1, 2)], slab_at(2)))
    fc.append(send(fpx.at[pl.ds(5, 2)], fpx.at[pl.ds(9, 2)], slab_at(-2)))

    banded(w_in, w_a, w_b, w_out, spread[...], wt, w1, w4, wf, tiles)
    for zb in range(NB):
        mask[zb * RY : zb * RY + 72] = jnp.ones((72, 128), F32)
        mask[zb * RY + 72 : zb * RY + RY] = jnp.zeros((8, 128), F32)
    held[3].wait()
    for X in range(2):
        fine, means = parts[X]
        targets = []
        for i, j in stress_pairs:
            t = mean([fine[i][n] * fine[j][n] for n in range(4)]) - means[i] * means[j]
            targets.append(jnp.concatenate([t, blank], axis=0).astype(BF))
        t = mm(jnp.concatenate(targets, axis=1), texp[...])
        for zb in range(8):
            tx[X, zb * RY : zb * RY + RY] = t[:, zb * 128 : zb * 128 + 128]
    for copy in uc:
        copy.wait_recv()
    vzf[1] = vzr[0] + vzr[1]
    for copy in fc:
        copy.wait_recv()
    vc = []
    for place, k in ((0, 1), (1, -1)):
        vc.append(send(vb, vbx.at[place], slab_at(k)))
        vc.append(send(vzf.at[1], vzf.at[2 * place], slab_at(k)))

    def expand(src, table, dst, count, shifts, start):
        width = src.shape[2]

        @pl.loop(0, count // 4)
        def _(q):
            r = mm(src[pl.ds(q * 4, 4)].reshape(4 * RY, width), table[...])
            for n in range(4):
                for zb in range(NB):
                    block = r[n * RY : n * RY + RY, zb * 128 : zb * 128 + 128]
                    for m, shift in enumerate(shifts):
                        moved = pltpu.roll(block, shift, 1) if shift else block
                        dst[lax.rem(q * 4 + start, 12) + n, zb * RY : zb * RY + RY, m * 128 : m * 128 + 128] = moved.astype(BF)

    held[2].wait()
    expand(fpx, fexp, xe0, 12, (0, 40, 80), 0)

    @pl.loop(0, 10)
    def _(p):
        write_plane(xe1, p, jnp.tanh(conv_plane(window_fields(xe0, p, ALL), w1[...])) * mask[...])

    for k, (src, dst, count) in enumerate(((xe1, xe2, 8), (xe2, xe3, 6))):

        @pl.loop(0, count)
        def _(p, src=src, dst=dst, k=k):
            write_plane(dst, p, jnp.tanh(conv_plane(window(src, p, ALL), wt[k])) * mask[...])

    held[4].wait()
    held[5].wait()
    for X in range(2):
        pred = (conv_plane(window(xe3, X + 1, ALL), wt[2]) * mask[...])[RY : RY + OWN]
        stress = pred.astype(BF)
        cot = (2.0 / SIZE * (pred - tx[X])).astype(BF)
        c4[X] = cot.astype(F32)
        for value, pack, edges, at in ((cot, cpx, ce, 3), (stress, spx, se, 2)):
            joined = jnp.concatenate([value[zb * RY : zb * RY + RY] for zb in range(8)], axis=1)
            pack[at + X, :, 0:384] = mm(joined, comp[...]).astype(BF)
            edges[0, X] = mm(value[7 * RY : 8 * RY], cedge[0]).astype(BF)
            edges[1, X] = mm(value[0:RY], cedge[1]).astype(BF)

    zc = []
    for side, k in ((0, 1), (1, -1)):
        zc.append(send(ce.at[side], cer.at[side], grp_at(k)))
        zc.append(send(se.at[side], ser.at[side], grp_at(k)))
    for copy in zc:
        copy.wait_recv()
    for X in range(2):
        cpx[3 + X, :, 384:512] = cer[0, X] + cer[1, X]
        spx[2 + X, :, 384:512] = ser[0, X] + ser[1, X]
    cc = []
    cc.append(send(cpx.at[pl.ds(3, 2)], cpx.at[pl.ds(1, 2)], slab_at(1)))
    cc.append(send(cpx.at[pl.ds(3, 2)], cpx.at[pl.ds(5, 2)], slab_at(-1)))
    cc.append(send(cpx.at[pl.ds(4, 1)], cpx.at[pl.ds(0, 1)], slab_at(2)))
    cc.append(send(cpx.at[pl.ds(3, 1)], cpx.at[pl.ds(7, 1)], slab_at(-2)))
    weight_gradient(xe3, 1, [c4[0], c4[1]], gsrc, 3, gtmp)

    for copy in vc:
        copy.wait_recv()
    pads = jnp.zeros((8, 128), F32)
    for c in range(3):

        @pl.loop(0, 12)
        def _(p, c=c):
            for t in range(2):
                vext[c, p, t, 0:8] = pads
                vext[c, p, t, 152:160] = pads

        @pl.loop(0, 8)
        def _(p, c=c):
            for t in range(2):
                fs[c, p, t, 0:8] = pads
                fs[c, p, t, 152:160] = pads

        for x in range(4):
            vext[c, x, 0, 8:152] = vbx[0, c, x].astype(F32)
            vext[c, 4 + x, 0, 8:152] = v[c, x]
            vext[c, 8 + x, 0, 8:152] = vbx[1, c, x].astype(F32)
    held[8].wait()
    for n in range(3):
        r = mm(vzf[n], vze[...])
        for c in range(3):
            for x in range(4):
                p = c * 4 + x
                vext[c, 4 * n + x, 1, 8:152] = r[:, p * 128 : p * 128 + 128]

    count = 48
    lane = lanes((count, 128))
    low = (lane < 1, lane < 2, lane >= 127, lane >= 126)

    @pl.loop(0, 8)
    def _(p):
        for t in range(2):
            for r in range(0, 144, count):
                vel, outs = stencil(vext, p + 2, t, r, count, low)
                for i in range(3):
                    fs[i, p, t, 8 + r : 8 + r + count] = vel[i] + outs[i]

    for copy in cc:
        copy.wait_recv()
    sc = []
    sc.append(send(spx.at[pl.ds(2, 2)], spx.at[pl.ds(0, 2)], slab_at(1)))
    sc.append(send(spx.at[pl.ds(2, 2)], spx.at[pl.ds(4, 2)], slab_at(-1)))
    wc = []
    for k in range(1, GRP):
        other = lax.rem(g + k, GRP)
        rows = pl.ds(pl.multiple_of(other * 16, 16), 32)
        wc.append(send(spx.at[pl.ds(2, 2), rows, pl.ds(0, 384)], sw.at[g], grp_at(k)))
    rows = pl.ds(pl.multiple_of(g * 16, 16), 32)
    sw[g] = spx[2:4, rows, 0:384]

    held[6].wait()
    expand(cpx, cexp, xe0, 8, (0, 60), 8)

    def damp(act, p):
        below = act[p, :, 0:128].astype(F32)
        return (1.0 - below * below) * mask[...]

    @pl.loop(0, 6)
    def _(p):
        write_plane(xe3, p, conv_plane(window_cot(xe0, p, ALL), w4[...]) * damp(xe3, p))

    def own(ref, at):
        return [ref[at + X, MID, 0:128].astype(F32) for X in range(2)]

    weight_gradient(xe2, 2, own(xe3, 2), gsrc, 2, gtmp)

    @pl.loop(0, 4)
    def _(p):
        write_plane(xe2, p + 2, conv_plane(window(xe3, p, ALL), wt[3]) * damp(xe2, p + 2))

    weight_gradient(xe1, 3, own(xe2, 3), gsrc, 1, gtmp)
    for X in range(2):
        c1[X] = (conv_plane(window(xe2, X + 2, ALL), wt[4]) * damp(xe1, X + 4))[MID].astype(BF).astype(F32)
    first_gradient(xe0, 4, [c1[0], c1[1]], gsrc, gtmp)

    first = [send(gsrc.at[peer_a(k)[0]], r1.at[k - 1], peer_a(k)[1]) for k in range(1, 16)]

    for copy in sc:
        copy.wait_recv()
    for n in (9, 10, 11):
        held[n].wait()
    for n in range(8):
        at = 1 + n // 2
        lower, mid, upper = (spx[at + d].astype(F32) for d in (-1, 0, 1))
        if n % 2 == 0:
            slope = 8.0 * mid - upper - 7.0 * lower
        else:
            slope = 7.0 * upper - 8.0 * mid + lower
        gxt[n * RY : n * RY + RY, 0:512] = slope.astype(BF)
        gxt[n * RY : n * RY + RY, 512:1024] = spx[at]
        if n % 2 == 0:
            r2s[n // 2] = mm(spx[at], q2[...]).astype(BF)
    r = mm(gxt[...], q1[...]).astype(BF)
    for n in range(8):
        both = jnp.concatenate([r[n * RY : n * RY + RY], r2s[n // 2]], axis=0)
        force[n] = mm(pb[...], both) * (-4.0 / 12.0)

    for copy in first:
        copy.wait_recv()
    total = gsrc[a]
    for k in range(15):
        total = total + r1[k]
    r2g[b] = total
    second = [send(r2g.at[b], r2g.at[b], peer_b(k)) for k in range(1, 8)]

    @pl.loop(0, 8)
    def _(p):
        for t in range(2):
            for i in range(3):
                at = i * 256 + t * 128
                fs[i, p, t, 8:152] = fs[i, p, t, 8:152] + 0.1 * force[p, :, at : at + 128]

    for copy in second:
        copy.wait_recv()
    total = r2g[0]
    for k in range(1, 8):
        total = total + r2g[k]
    gout[a] = total
    third = [send(gout.at[a], gout.at[a], peer_a(k)[1]) for k in range(1, 16)]

    @pl.loop(0, 4)
    def _(x):
        for r in range(0, 144, count):
            vel, outs = stencil(fs, x + 2, 0, r, count, low)
            for i in range(3):
                again = outs[i] + 0.1 * force[x + 2, r : r + count, i * 256 : i * 256 + 128]
                vnext[i, x, r : r + count] = 0.5 * (v[i, x, r : r + count] + vel[i] + again)

    for copy in third:
        copy.wait_recv()
    for copy in wc:
        copy.wait_recv()
    for copy in sent:
        copy.wait_send()


def finish(vnext, sw, gout, vout, stress, g0, g1, g2, g3, rows):
    vout[...] = vnext[...]
    start = 2 * lax.axis_index("grp")
    low = lanes((18, 128)) < 64
    for tile in range(3):
        rows[tile] = sw[:, :, :, tile * 128 : tile * 128 + 128].astype(F32)
    for x in range(2):
        for c in range(6):
            for half in range(2):
                left = rows[c // 2, 2 * half, x, pl.ds(start, 18), :]
                right = rows[c // 2, 2 * half + 1, x, pl.ds(start, 18), :]
                if c % 2:
                    left = pltpu.roll(left, 64, 1)
                else:
                    right = pltpu.roll(right, 64, 1)
                stress[c, x, :, half * 128 : half * 128 + 128] = jnp.where(low, left, right).astype(BF)
    for layer, out in enumerate((g0, g1, g2, g3)):
        for tap in range(27):
            at = tap % 8 * 16
            out[tap] = gout[layer * 4 + tap // 8, 0 : out.shape[1], at : at + out.shape[2]]


def local(velocity, w_in, w_mid_a, w_mid_b, w_out):
    vm = pltpu.VMEM
    scratch = [
        vm((12, RY, 256), BF), vm((2, 2, RY, 128), BF), vm((2, 2, RY, 128), BF),
        vm((3, 4, 144, 128), BF), vm((2, 3, 4, 144, 128), BF),
        vm((2, 144, 128), BF), vm((2, 144, 128), BF), vm((3, 144, 128), BF),
        vm((2, OWN, 128), F32), vm((5, 512, 384), BF),
        vm((128, 384), BF), vm((256, 384), BF), vm((256, 384), F32), vm((27, 16, 128), F32),
        vm((12, ROWS, 384), BF), vm((10, ROWS, 512), BF), vm((8, ROWS, 512), BF), vm((6, ROWS, 512), BF),
        vm((2, OWN, 128), F32),
        vm((2, OWN, 128), F32),
        vm((ROWS, 128), F32),
        vm((8, RY, 512), BF), vm((6, RY, 512), BF),
        vm((2, 2, RY, 128), BF), vm((2, 2, RY, 128), BF), vm((2, 2, RY, 128), BF), vm((2, 2, RY, 128), BF),
        vm((8 * RY, 1024), BF), vm((4, RY, 768), BF), vm((8, 144, 768), F32),
        vm((3, 12, 2, 160, 128), F32), vm((3, 8, 2, 160, 128), F32),
        vm((384, 512), F32), vm((16, 16, 128), F32), vm((15, 16, 128), F32), vm((8, 16, 128), F32),
        pltpu.SemaphoreType.DMA((12,)), pltpu.SemaphoreType.DMA((64,)), pltpu.SemaphoreType.DMA((64,)),
    ]
    *consts, spread = tables()
    scratch = [vm(t.shape, BF) for t in consts] + scratch
    inside = pl.BlockSpec(memory_space=pltpu.VMEM)
    vnext, sw, gout = pl.pallas_call(
        body,
        out_shape=[
            jax.ShapeDtypeStruct((3, 4, 144, 128), F32),
            jax.ShapeDtypeStruct((4, 2, 32, 384), BF),
            jax.ShapeDtypeStruct((16, 16, 128), F32),
        ],
        in_specs=[inside] * 6 + [pl.BlockSpec(memory_space=pl.ANY)] * len(consts),
        out_specs=[inside] * 3,
        scratch_shapes=scratch,
        compiler_params=pltpu.CompilerParams(
            collective_id=0, has_side_effects=True, vmem_limit_bytes=62 * 1024 * 1024
        ),
    )(velocity, w_in, w_mid_a, w_mid_b, w_out, spread, *consts)
    shapes = [((3, 4, 144, 128), F32), ((6, 2, 18, 256), BF)]
    shapes += [((27, 16, 3), F32), ((27, 16, 16), F32), ((27, 16, 16), F32), ((27, 6, 16), F32)]
    return tuple(
        pl.pallas_call(
            finish,
            out_shape=[jax.ShapeDtypeStruct(*shape) for shape in shapes],
            in_specs=[inside] * 3,
            out_specs=[inside] * 6,
            scratch_shapes=[vm((3, 4, 2, 32, 128), F32)],
            compiler_params=pltpu.CompilerParams(vmem_limit_bytes=32 * 1024 * 1024),
        )(vnext, sw, gout)
    )


def solution(mesh):
    in_specs = (P(None, "slab", None, "grp"), P(), P(), P(), P())
    out_specs = (P(None, "slab", None, "grp"), P(None, "slab", "grp", None), P(), P(), P(), P())
    return jax.shard_map(local, mesh=mesh, in_specs=in_specs, out_specs=out_specs, check_vma=False)
```

time: 126 us -> 99.4 us (0.79)
  Pallas kernels: 111 us -> 85 us
    pallas_call x1, Pallas kernels: 111 us -> 83.8 us  [local(): pl.pallas_call(body, out_shape=[jax.ShapeDtypeStruct((3, 4, 144, 128), F3...]
    unnamed x18 -> x10, local copies, waits for them, and re-layouts: 3.36 us -> 9.39 us
    pallas_call x0 -> x5, local copies, waits for them, and re-layouts: none -> 3.93 us  [local(): pl.pallas_call(finish, out_shape=[jax.ShapeDtypeStruct(*shape) for shape...]
    transpose x6 -> x0, local copies, waits for them, and re-layouts: 3.27 us -> none  [the longest x5 3.15 us: forward_rows(): return jnp.transpose(padded, (0, 2, 1)).reshape(432, 16)]
    another operation x9 -> x0, local copies, waits for them, and re-layouts: 2.41 us -> none  [local(): jnp.stack([forward_rows(w) for w in (w_in, w_mid_a, w_mid_b, w_out)] + [b...]
    reshape x3 -> x0, local copies, waits for them, and re-layouts: 1.39 us -> none  [the longest x1 0.85 us: local(): stress = jnp.transpose(window, (3, 1, 2, 0, 4)).reshape(6, 2, 18, 256)]
where the time goes in v2:
time: 99.4 us; the launch traced here: 99 us
  Pallas kernels  85 us (86%)
  local copies, waits for them, and re-layouts  13.3 us (13%)
    pallas_call x1, Pallas kernels, local(): pl.pallas_call(body, out_shape=[jax.ShapeDtypeStruct((3, 4, 144, 128), F3...  83.8 us
    unnamed x10, local copies, waits for them, and re-layouts  9.39 us
    pallas_call x5, local copies, waits for them, and re-layouts, local(): pl.pallas_call(finish, out_shape=[jax.ShapeDtypeStruct(*shape) for shape...  3.93 us

profile of v2, /device:TPU:1, one launch (start us, length us, event | category | flops | bytes accessed | tf_op | source)
XLA Modules:
  0.0 99.0 jit_solution(14191901025371195082)
XLA Ops:
  0.6 1.5 %copy.27.w_out = bf16[27,6,16]{2,1,0:T(8,128)(2,1)} copy(bf16[27,6,16]{0,2,1:T(8,128)(2,1)} %param.22) | data formatting | bytes 10368 | tf_op args[4]
  2.1 1.6 %copy.24.w_in = bf16[27,16,3]{2,1,0:T(8,128)(2,1)} copy(bf16[27,16,3]{0,1,2:T(8,128)(2,1)} %param.19) | data formatting | bytes 5184 | tf_op args[1]
  3.7 1.7 %copy.25.w_a = bf16[27,16,16]{2,1,0:T(8,128)(2,1)} copy(bf16[27,16,16]{0,2,1:T(8,128)(2,1)} %param.20) | data formatting | bytes 27648 | tf_op args[2]
  5.4 1.7 %copy.26.w_b = bf16[27,16,16]{2,1,0:T(8,128)(2,1)} copy(bf16[27,16,16]{0,2,1:T(8,128)(2,1)} %param.21) | data formatting | bytes 27648 | tf_op args[3]
  7.0 83.8 %shard_map.217 = (f32[3,4,144,128]{3,2,1,0:T(8,128)}, bf16[4,2,32,384]{3,2,1,0:T(8,128)(2,1)}, f32[16,16,128]{2,1,0:T(8,128)}) custom-call(f32[3,4,144,128]{3,2,1,0:T(8,128)} %v.1, bf16[27,16,3]{2,1,0:T(8,128)(2,1)} %copy.24.w_in, bf16[27,16,16]{2,1,0:T(8,128)(2,1)} %copy.25.w_a, bf16[27,16,16]{2,1,0:T(8,128)(2,1)} %copy.26.w_b, ...), custom_call_target="tpu_custom_call" | custom-call | tf_op jit(solution)/shard_map/pallas_call | solution.py:633
  90.8 0.0 copy-start
  90.8 1.2 %copy-done = f32[3,4,144,128]{3,2,1,0:T(8,128)S(1)} copy-done((f32[3,4,144,128]{3,2,1,0:T(8,128)S(1)}, f32[3,4,144,128]{3,2,1,0:T(8,128)}, u32[]{:S(2)}) %copy-start) | copy-done | bytes 884760
  92.0 0.0 copy-start.1
  92.0 0.9 copy-done.1
  92.9 0.0 copy-start.2
  92.9 0.9 copy-done.2
  93.8 1.2 %shard_map.218 = (f32[3,4,144,128]{3,2,1,0:T(8,128)}, bf16[6,2,18,256]{3,2,1,0:T(8,128)(2,1)S(1)}, f32[27,16,3]{2,1,0:T(8,128)S(1)}, f32[27,16,16]{2,1,0:T(8,128...) custom-call(f32[3,4,144,128]{3,2,1,0:T(8,128)S(1)} %copy-done, bf16[4,2,32,384]{3,2,1,0:T(8,128)(2,1)S(1)} %copy-done.1, ...), custom_call_target="tpu_custom_call" | custom-call | tf_op jit(solution)/shard_map/pallas_call | solution.py:650
  95.0 0.8 copy.29
  95.8 0.7 copy.32
  96.6 0.7 copy.28
  97.3 0.8 copy.30
  98.1 0.8 copy.31
Async XLA Ops:
  90.8 1.2 %copy-start = (f32[3,4,144,128]{3,2,1,0:T(8,128)S(1)}, f32[3,4,144,128]{3,2,1,0:T(8,128)}, u32[]{:S(2)}) copy-start(f32[3,4,144,128]{3,2,1,0:T(8,128)} %get-tuple-element.9.vnext) | copy-start | bytes 2654212
  92.0 0.9 copy-start.1
  92.9 0.9 copy-start.2

commit v3 on v2

--- a/solution.py
+++ b/solution.py
@@ -138,18 +138,29 @@
 
 def conv_plane(lhs, kernel):
     r = mm(lhs, kernel)
-    return pltpu.roll(r[:, 0:128], 1, 0) + r[:, 128:256] + pltpu.roll(r[:, 256:384], ROWS - 1, 0)
+    return pltpu.roll(r[:, 0:128], 1, 0) + r[:, 128:256] + pltpu.roll(r[:, 256:384], r.shape[0] - 1, 0)
 
 
 ALL = slice(0, ROWS)
 MID = slice(RY, RY + OWN)
 
 
-def banded(w_in, w_a, w_b, w_out, spread, wt, w1, w4, wf, tiles):
+def banded(w_in, w_a, w_b, w_out, spread, wt, w1, w4, wf, tiles, flat, turned):
     group = lanes((16, 128)) // 16
 
-    def turned(w, tap):
-        return lax.dot_general(w[tap], spread[0 : w.shape[1]], (((0,), (0,)), ((), ())), preferred_element_type=F32)
+    def load(w):
+        flat[...] = jnp.zeros((256, 128), F32)
+        for n in range(w.shape[0]):
+            flat[n * 16 : n * 16 + 16, 0:27] = w[n].astype(F32)
+
+    def turn(first, count, backwards):
+        for n in range(count):
+            rows = flat[n * 16 : n * 16 + 16] if first else flat[pl.ds(n, 16, stride=16), :]
+            turned[n * 32 : n * 32 + 32] = lax.dot_general(
+                rows[:, 0:32].astype(BF), spread, (((0,), (0,)), ((), ())), preferred_element_type=F32
+            )
+        for tap in range(27):
+            tiles[tap] = turned[pl.ds(26 - tap if backwards else tap, 16, stride=32), :]
 
     def fill(out):
         for dx in range(3):
@@ -163,15 +174,6 @@
                     wt[out, row : row + 16, at] = value.astype(BF)
         wt[out, 464:496] = jnp.zeros((32, 384), BF)
 
-    for out, w in enumerate((w_a, w_b, w_out)):
-        for tap in range(27):
-            tiles[tap] = turned(w, tap)
-        fill(out)
-    for out, w in ((3, w_b), (4, w_a)):
-        for tap in range(27):
-            tiles[tap] = mm(w[26 - tap], spread)
-        fill(out)
-
     def small(count, starts):
         wf[...] = jnp.zeros((256, 384), F32)
         part = lanes((count, 128)) // 16
@@ -184,13 +186,24 @@
                     row = starts[dx] + kz * count
                     wf[row : row + count, dy * 128 : dy * 128 + 128] = value
 
-    for tap in range(27):
-        tiles[tap, 0:3] = turned(w_in, tap)
-        tiles[tap, 3:4] = jnp.zeros((1, 128), F32)
+    load(w_in)
+    turn(True, 4, False)
     small(4, (0, 40, 80))
     w1[...] = wf[0:128].astype(BF)
-    for tap in range(27):
-        tiles[tap, 0:6] = mm(w_out[26 - tap], spread)
+    load(w_a)
+    turn(False, 16, False)
+    fill(0)
+    turn(True, 16, True)
+    fill(4)
+    load(w_b)
+    turn(False, 16, False)
+    fill(1)
+    turn(True, 16, True)
+    fill(3)
+    load(w_out)
+    turn(False, 16, False)
+    fill(2)
+    turn(True, 6, True)
     small(6, (0, 60, 128))
     w4[...] = wf[...].astype(BF)
 
@@ -282,7 +295,7 @@
     near = refs[15:27]
     fsel, fedge, fexp, texp, comp, cedge, cexp, vz, vze, pb, q1, q2 = near
     (
-        fpx, fe, fer, vb, vbx, vzs, vzr, vzf, tx, wt, w1, w4, wf, tiles, xe0, xe1, xe2, xe3, c4, c1, mask,
+        fpx, fe, fer, vb, vbx, vzs, vzr, vzf, tx, wt, w1, w4, wf, tiles, flat, turned, xe0, xe1, xe2, xe3, c4, c1, mask,
         cpx, spx, ce, cer, se, ser, gxt, r2s, force, vext, fs, gtmp, gsrc, r1, r2g, csem, ssem, rsem,
     ) = refs[27:]
     held = [pltpu.make_async_copy(far[n], near[n], csem.at[n]) for n in range(12)]
@@ -348,6 +361,14 @@
     pl.semaphore_wait(barrier, len(friends))
     zc = [send(fe.at[side], fer.at[side], grp_at(k)) for side, k in ((0, 1), (1, -1))]
 
+    fc = []
+    fc.append(send(fpx.at[pl.ds(5, 2), :, pl.ds(0, 128)], fpx.at[pl.ds(3, 2), :, pl.ds(0, 128)], slab_at(1)))
+    fc.append(send(fpx.at[pl.ds(5, 2), :, pl.ds(0, 128)], fpx.at[pl.ds(7, 2), :, pl.ds(0, 128)], slab_at(-1)))
+    fc.append(send(fpx.at[pl.ds(6, 1), :, pl.ds(0, 128)], fpx.at[pl.ds(0, 1), :, pl.ds(0, 128)], slab_at(3)))
+    fc.append(send(fpx.at[pl.ds(5, 1), :, pl.ds(0, 128)], fpx.at[pl.ds(11, 1), :, pl.ds(0, 128)], slab_at(-3)))
+    fc.append(send(fpx.at[pl.ds(5, 2), :, pl.ds(0, 128)], fpx.at[pl.ds(1, 2), :, pl.ds(0, 128)], slab_at(2)))
+    fc.append(send(fpx.at[pl.ds(5, 2), :, pl.ds(0, 128)], fpx.at[pl.ds(9, 2), :, pl.ds(0, 128)], slab_at(-2)))
+
     vb[...] = v[...].astype(BF)
     held[7].wait()
     joined = jnp.concatenate([vb[c, x] for c in range(3) for x in range(4)], axis=1)
@@ -359,15 +380,14 @@
         copy.wait_recv()
     for X in range(2):
         fpx[5 + X, :, 128:256] = fpx[5 + X, :, 128:256] + fer[0, X] + fer[1, X]
-    fc = []
-    fc.append(send(fpx.at[pl.ds(5, 2)], fpx.at[pl.ds(3, 2)], slab_at(1)))
-    fc.append(send(fpx.at[pl.ds(5, 2)], fpx.at[pl.ds(7, 2)], slab_at(-1)))
-    fc.append(send(fpx.at[pl.ds(6, 1)], fpx.at[pl.ds(0, 1)], slab_at(3)))
-    fc.append(send(fpx.at[pl.ds(5, 1)], fpx.at[pl.ds(11, 1)], slab_at(-3)))
-    fc.append(send(fpx.at[pl.ds(5, 2)], fpx.at[pl.ds(1, 2)], slab_at(2)))
-    fc.append(send(fpx.at[pl.ds(5, 2)], fpx.at[pl.ds(9, 2)], slab_at(-2)))
-
-    banded(w_in, w_a, w_b, w_out, spread[...], wt, w1, w4, wf, tiles)
+    fc.append(send(fpx.at[pl.ds(5, 2), :, pl.ds(128, 128)], fpx.at[pl.ds(3, 2), :, pl.ds(128, 128)], slab_at(1)))
+    fc.append(send(fpx.at[pl.ds(5, 2), :, pl.ds(128, 128)], fpx.at[pl.ds(7, 2), :, pl.ds(128, 128)], slab_at(-1)))
+    fc.append(send(fpx.at[pl.ds(6, 1), :, pl.ds(128, 128)], fpx.at[pl.ds(0, 1), :, pl.ds(128, 128)], slab_at(3)))
+    fc.append(send(fpx.at[pl.ds(5, 1), :, pl.ds(128, 128)], fpx.at[pl.ds(11, 1), :, pl.ds(128, 128)], slab_at(-3)))
+    fc.append(send(fpx.at[pl.ds(5, 2), :, pl.ds(128, 128)], fpx.at[pl.ds(1, 2), :, pl.ds(128, 128)], slab_at(2)))
+    fc.append(send(fpx.at[pl.ds(5, 2), :, pl.ds(128, 128)], fpx.at[pl.ds(9, 2), :, pl.ds(128, 128)], slab_at(-2)))
+
+    banded(w_in, w_a, w_b, w_out, spread[...], wt, w1, w4, wf, tiles, flat, turned)
     for zb in range(NB):
         mask[zb * RY : zb * RY + 72] = jnp.ones((72, 128), F32)
         mask[zb * RY + 72 : zb * RY + RY] = jnp.zeros((8, 128), F32)
@@ -381,6 +401,24 @@
         t = mm(jnp.concatenate(targets, axis=1), texp[...])
         for zb in range(8):
             tx[X, zb * RY : zb * RY + RY] = t[:, zb * 128 : zb * 128 + 128]
+    pads = jnp.zeros((8, 128), F32)
+    for c in range(3):
+
+        @pl.loop(0, 12)
+        def _(p, c=c):
+            for t in range(2):
+                vext[c, p, t, 0:8] = pads
+                vext[c, p, t, 152:160] = pads
+
+        @pl.loop(0, 8)
+        def _(p, c=c):
+            for t in range(2):
+                fs[c, p, t, 0:8] = pads
+                fs[c, p, t, 152:160] = pads
+
+        for x in range(4):
+            vext[c, 4 + x, 0, 8:152] = v[c, x]
+
     for copy in uc:
         copy.wait_recv()
     vzf[1] = vzr[0] + vzr[1]
@@ -420,7 +458,7 @@
     held[4].wait()
     held[5].wait()
     for X in range(2):
-        pred = (conv_plane(window(xe3, X + 1, ALL), wt[2]) * mask[...])[RY : RY + OWN]
+        pred = conv_plane(window(xe3, X + 1, MID), wt[2]) * mask[MID]
         stress = pred.astype(BF)
         cot = (2.0 / SIZE * (pred - tx[X])).astype(BF)
         c4[X] = cot.astype(F32)
@@ -434,38 +472,28 @@
     for side, k in ((0, 1), (1, -1)):
         zc.append(send(ce.at[side], cer.at[side], grp_at(k)))
         zc.append(send(se.at[side], ser.at[side], grp_at(k)))
+    cc = []
+    cc.append(send(cpx.at[pl.ds(3, 2), :, pl.ds(0, 384)], cpx.at[pl.ds(1, 2), :, pl.ds(0, 384)], slab_at(1)))
+    cc.append(send(cpx.at[pl.ds(3, 2), :, pl.ds(0, 384)], cpx.at[pl.ds(5, 2), :, pl.ds(0, 384)], slab_at(-1)))
+    cc.append(send(cpx.at[pl.ds(4, 1), :, pl.ds(0, 384)], cpx.at[pl.ds(0, 1), :, pl.ds(0, 384)], slab_at(2)))
+    cc.append(send(cpx.at[pl.ds(3, 1), :, pl.ds(0, 384)], cpx.at[pl.ds(7, 1), :, pl.ds(0, 384)], slab_at(-2)))
+    weight_gradient(xe3, 1, [c4[0], c4[1]], gsrc, 3, gtmp)
+
     for copy in zc:
         copy.wait_recv()
     for X in range(2):
         cpx[3 + X, :, 384:512] = cer[0, X] + cer[1, X]
         spx[2 + X, :, 384:512] = ser[0, X] + ser[1, X]
-    cc = []
-    cc.append(send(cpx.at[pl.ds(3, 2)], cpx.at[pl.ds(1, 2)], slab_at(1)))
-    cc.append(send(cpx.at[pl.ds(3, 2)], cpx.at[pl.ds(5, 2)], slab_at(-1)))
-    cc.append(send(cpx.at[pl.ds(4, 1)], cpx.at[pl.ds(0, 1)], slab_at(2)))
-    cc.append(send(cpx.at[pl.ds(3, 1)], cpx.at[pl.ds(7, 1)], slab_at(-2)))
-    weight_gradient(xe3, 1, [c4[0], c4[1]], gsrc, 3, gtmp)
+    cc.append(send(cpx.at[pl.ds(3, 2), :, pl.ds(384, 128)], cpx.at[pl.ds(1, 2), :, pl.ds(384, 128)], slab_at(1)))
+    cc.append(send(cpx.at[pl.ds(3, 2), :, pl.ds(384, 128)], cpx.at[pl.ds(5, 2), :, pl.ds(384, 128)], slab_at(-1)))
+    cc.append(send(cpx.at[pl.ds(4, 1), :, pl.ds(384, 128)], cpx.at[pl.ds(0, 1), :, pl.ds(384, 128)], slab_at(2)))
+    cc.append(send(cpx.at[pl.ds(3, 1), :, pl.ds(384, 128)], cpx.at[pl.ds(7, 1), :, pl.ds(384, 128)], slab_at(-2)))
 
     for copy in vc:
         copy.wait_recv()
-    pads = jnp.zeros((8, 128), F32)
     for c in range(3):
-
-        @pl.loop(0, 12)
-        def _(p, c=c):
-            for t in range(2):
-                vext[c, p, t, 0:8] = pads
-                vext[c, p, t, 152:160] = pads
-
-        @pl.loop(0, 8)
-        def _(p, c=c):
-            for t in range(2):
-                fs[c, p, t, 0:8] = pads
-                fs[c, p, t, 152:160] = pads
-
         for x in range(4):
             vext[c, x, 0, 8:152] = vbx[0, c, x].astype(F32)
-            vext[c, 4 + x, 0, 8:152] = v[c, x]
             vext[c, 8 + x, 0, 8:152] = vbx[1, c, x].astype(F32)
     held[8].wait()
     for n in range(3):
@@ -479,14 +507,16 @@
     lane = lanes((count, 128))
     low = (lane < 1, lane < 2, lane >= 127, lane >= 126)
 
-    @pl.loop(0, 8)
-    def _(p):
-        for t in range(2):
-            for r in range(0, 144, count):
-                vel, outs = stencil(vext, p + 2, t, r, count, low)
-                for i in range(3):
-                    fs[i, p, t, 8 + r : 8 + r + count] = vel[i] + outs[i]
-
+    def first_step(start, stop):
+        @pl.loop(start, stop)
+        def _(p):
+            for t in range(2):
+                for r in range(0, 144, count):
+                    vel, outs = stencil(vext, p + 2, t, r, count, low)
+                    for i in range(3):
+                        fs[i, p, t, 8 + r : 8 + r + count] = vel[i] + outs[i]
+
+    first_step(0, 3)
     for copy in cc:
         copy.wait_recv()
     sc = []
@@ -503,9 +533,9 @@
     held[6].wait()
     expand(cpx, cexp, xe0, 8, (0, 60), 8)
 
-    def damp(act, p):
-        below = act[p, :, 0:128].astype(F32)
-        return (1.0 - below * below) * mask[...]
+    def damp(act, p, rows=ALL):
+        below = act[p, rows, 0:128].astype(F32)
+        return (1.0 - below * below) * mask[rows]
 
     @pl.loop(0, 6)
     def _(p):
@@ -522,10 +552,19 @@
 
     weight_gradient(xe1, 3, own(xe2, 3), gsrc, 1, gtmp)
     for X in range(2):
-        c1[X] = (conv_plane(window(xe2, X + 2, ALL), wt[4]) * damp(xe1, X + 4))[MID].astype(BF).astype(F32)
+        c1[X] = (conv_plane(window(xe2, X + 2, MID), wt[4]) * damp(xe1, X + 4, MID)).astype(BF).astype(F32)
     first_gradient(xe0, 4, [c1[0], c1[1]], gsrc, gtmp)
 
     first = [send(gsrc.at[peer_a(k)[0]], r1.at[k - 1], peer_a(k)[1]) for k in range(1, 16)]
+
+    first_step(3, 8)
+    for copy in first:
+        copy.wait_recv()
+    total = gsrc[a]
+    for k in range(15):
+        total = total + r1[k]
+    r2g[b] = total
+    second = [send(r2g.at[b], r2g.at[b], peer_b(k)) for k in range(1, 8)]
 
     for copy in sc:
         copy.wait_recv()
@@ -547,13 +586,13 @@
         both = jnp.concatenate([r[n * RY : n * RY + RY], r2s[n // 2]], axis=0)
         force[n] = mm(pb[...], both) * (-4.0 / 12.0)
 
-    for copy in first:
-        copy.wait_recv()
-    total = gsrc[a]
-    for k in range(15):
-        total = total + r1[k]
-    r2g[b] = total
-    second = [send(r2g.at[b], r2g.at[b], peer_b(k)) for k in range(1, 8)]
+    for copy in second:
+        copy.wait_recv()
+    total = r2g[0]
+    for k in range(1, 8):
+        total = total + r2g[k]
+    gout[a] = total
+    third = [send(gout.at[a], gout.at[a], peer_a(k)[1]) for k in range(1, 16)]
 
     @pl.loop(0, 8)
     def _(p):
@@ -561,14 +600,6 @@
             for i in range(3):
                 at = i * 256 + t * 128
                 fs[i, p, t, 8:152] = fs[i, p, t, 8:152] + 0.1 * force[p, :, at : at + 128]
-
-    for copy in second:
-        copy.wait_recv()
-    total = r2g[0]
-    for k in range(1, 8):
-        total = total + r2g[k]
-    gout[a] = total
-    third = [send(gout.at[a], gout.at[a], peer_a(k)[1]) for k in range(1, 16)]
 
     @pl.loop(0, 4)
     def _(x):
@@ -586,26 +617,36 @@
         copy.wait_send()
 
 
-def finish(vnext, sw, gout, vout, stress, g0, g1, g2, g3, rows):
+def finish(vnext, sw, gout, vout, stress, g0, g1, g2, g3, rows, taps):
     vout[...] = vnext[...]
     start = 2 * lax.axis_index("grp")
     low = lanes((18, 128)) < 64
     for tile in range(3):
         rows[tile] = sw[:, :, :, tile * 128 : tile * 128 + 128].astype(F32)
-    for x in range(2):
-        for c in range(6):
-            for half in range(2):
+    for c in range(6):
+        for half in range(2):
+            planes = []
+            for x in range(2):
                 left = rows[c // 2, 2 * half, x, pl.ds(start, 18), :]
                 right = rows[c // 2, 2 * half + 1, x, pl.ds(start, 18), :]
                 if c % 2:
                     left = pltpu.roll(left, 64, 1)
                 else:
                     right = pltpu.roll(right, 64, 1)
-                stress[c, x, :, half * 128 : half * 128 + 128] = jnp.where(low, left, right).astype(BF)
+                planes.append(jnp.where(low, left, right))
+            stress[c, :, :, half * 128 : half * 128 + 128] = jnp.stack(planes, axis=1).astype(BF)
     for layer, out in enumerate((g0, g1, g2, g3)):
         for tap in range(27):
-            at = tap % 8 * 16
-            out[tap] = gout[layer * 4 + tap // 8, 0 : out.shape[1], at : at + out.shape[2]]
+            tile = gout[layer * 4 + tap // 8]
+            shift = (128 - tap % 8 * 16) % 128
+            taps[tap * 16 : tap * 16 + 16] = pltpu.roll(tile, shift, 1) if shift else tile
+        for n in range(16 if layer == 0 else out.shape[0]):
+            turned = jnp.transpose(taps[pl.ds(n, 32, stride=16), :])
+            if layer == 0:
+                for q in range(3):
+                    out[q, n : n + 1] = turned[q : q + 1, 0:27]
+            else:
+                out[n] = turned[0:16, 0:27]
 
 
 def local(velocity, w_in, w_mid_a, w_mid_b, w_out):
@@ -616,6 +657,7 @@
         vm((2, 144, 128), BF), vm((2, 144, 128), BF), vm((3, 144, 128), BF),
         vm((2, OWN, 128), F32), vm((5, 512, 384), BF),
         vm((128, 384), BF), vm((256, 384), BF), vm((256, 384), F32), vm((27, 16, 128), F32),
+        vm((256, 128), F32), vm((512, 128), F32),
         vm((12, ROWS, 384), BF), vm((10, ROWS, 512), BF), vm((8, ROWS, 512), BF), vm((6, ROWS, 512), BF),
         vm((2, OWN, 128), F32),
         vm((2, OWN, 128), F32),
@@ -625,7 +667,7 @@
         vm((8 * RY, 1024), BF), vm((4, RY, 768), BF), vm((8, 144, 768), F32),
         vm((3, 12, 2, 160, 128), F32), vm((3, 8, 2, 160, 128), F32),
         vm((384, 512), F32), vm((16, 16, 128), F32), vm((15, 16, 128), F32), vm((8, 16, 128), F32),
-        pltpu.SemaphoreType.DMA((12,)), pltpu.SemaphoreType.DMA((64,)), pltpu.SemaphoreType.DMA((64,)),
+        pltpu.SemaphoreType.DMA((12,)), pltpu.SemaphoreType.DMA((80,)), pltpu.SemaphoreType.DMA((80,)),
     ]
     *consts, spread = tables()
     scratch = [vm(t.shape, BF) for t in consts] + scratch
@@ -643,19 +685,25 @@
         compiler_params=pltpu.CompilerParams(
             collective_id=0, has_side_effects=True, vmem_limit_bytes=62 * 1024 * 1024
         ),
-    )(velocity, w_in, w_mid_a, w_mid_b, w_out, spread, *consts)
-    shapes = [((3, 4, 144, 128), F32), ((6, 2, 18, 256), BF)]
-    shapes += [((27, 16, 3), F32), ((27, 16, 16), F32), ((27, 16, 16), F32), ((27, 6, 16), F32)]
-    return tuple(
-        pl.pallas_call(
-            finish,
-            out_shape=[jax.ShapeDtypeStruct(*shape) for shape in shapes],
-            in_specs=[inside] * 3,
-            out_specs=[inside] * 6,
-            scratch_shapes=[vm((3, 4, 2, 32, 128), F32)],
-            compiler_params=pltpu.CompilerParams(vmem_limit_bytes=32 * 1024 * 1024),
-        )(vnext, sw, gout)
+    )(
+        velocity,
+        jnp.transpose(w_in, (2, 1, 0)),
+        *(jnp.transpose(w, (1, 2, 0)) for w in (w_mid_a, w_mid_b, w_out)),
+        spread,
+        *consts,
     )
+    shapes = [((3, 4, 144, 128), F32), ((6, 18, 2, 256), BF)]
+    shapes += [((3, 16, 27), F32), ((16, 16, 27), F32), ((16, 16, 27), F32), ((6, 16, 27), F32)]
+    vnext, stress, g0, *rest = pl.pallas_call(
+        finish,
+        out_shape=[jax.ShapeDtypeStruct(*shape) for shape in shapes],
+        in_specs=[inside] * 3,
+        out_specs=[inside] * 6,
+        scratch_shapes=[vm((3, 4, 2, 32, 128), F32), vm((512, 128), F32)],
+        compiler_params=pltpu.CompilerParams(vmem_limit_bytes=60 * 1024 * 1024),
+    )(vnext, sw, gout)
+    stress = jnp.transpose(stress, (0, 2, 1, 3))
+    return (vnext, stress, jnp.transpose(g0, (2, 1, 0)), *(jnp.transpose(g, (2, 0, 1)) for g in rest))
 
 
 def solution(mesh):

time: 99.4 us -> 85.3 us (0.86)
  local copies, waits for them, and re-layouts: 13.3 us -> 0 us
    unnamed x10 -> x0, local copies, waits for them, and re-layouts: 9.39 us -> none
    pallas_call x5 -> x0, local copies, waits for them, and re-layouts: 3.93 us -> none  [local(): pl.pallas_call(finish, out_shape=[jax.ShapeDtypeStruct(*shape) for shape...]
    pallas_call x1, Pallas kernels: 83.8 us -> 81.4 us  [local(): pl.pallas_call(body, out_shape=[jax.ShapeDtypeStruct((3, 4, 144, 128), F3...]
    pallas_call x1, Pallas kernels: 1.19 us -> 3.04 us  [local(): pl.pallas_call(finish, out_shape=[jax.ShapeDtypeStruct(*shape) for shape...]
where the time goes in v3:
time: 85.3 us; the launch traced here: 85.1 us
  Pallas kernels  84.5 us (99%)
    pallas_call x1, Pallas kernels, local(): pl.pallas_call(body, out_shape=[jax.ShapeDtypeStruct((3, 4, 144, 128), F3...  81.4 us
    pallas_call x1, Pallas kernels, local(): pl.pallas_call(finish, out_shape=[jax.ShapeDtypeStruct(*shape) for shape...  3.04 us

profile of v3, /device:TPU:1, one launch (start us, length us, event | category | flops | bytes accessed | tf_op | source)
XLA Modules:
  0.0 85.1 jit_solution(5171551450141331670)
XLA Ops:
  0.6 81.4 %shard_map.217 = (f32[3,4,144,128]{3,2,1,0:T(8,128)}, bf16[4,2,32,384]{3,2,1,0:T(8,128)(2,1)}, f32[16,16,128]{2,1,0:T(8,128)}) custom-call(f32[3,4,144,128]{3,2,1,0:T(8,128)} %v.1, bf16[3,16,27]{2,1,0:T(8,128)(2,1)} %bitcast.12, bf16[16,16,27]{2,1,0:T(8,128)(2,1)} %bitcast.9, bf16[16,16,27]{2,1,0:T(8,128)(2,1)} %bitcast.10, bf16[6,16,27]{2,1,0:T(8,128)(2,1)} %bitcast.11, ...), custom_call_target="tpu_custom_call" | custom-call | tf_op jit(solution)/shard_map/pallas_call | solution.py:675
  82.1 3.0 %shard_map.218 = (f32[3,4,144,128]{3,2,1,0:T(8,128)}, bf16[6,18,2,256]{3,2,1,0:T(2,128)(2,1)}, f32[3,16,27]{2,1,0:T(8,128)}, f32[16,16,27]{2,1,0:T(8,128)}, f32[16,16,27]{2,1,0:T(8,128)}, /*index=5*/f32[6,16,27]{2,1,0:T(8,128)}) custom-call(f32[3,4,144,128]{3,2,1,0:T(8,128)} %get-tuple-element.15.vnext, bf16[4,2,32,384]{3,2,1,0:T(8,128)(2,1)} %get-tuple-element.16.sw, ...), custom_call_target="tpu_custom_call" | custom-call | tf_op jit(solution)/shard_map/pallas_call | solution.py:697

commit v4 on v3

--- a/solution.py
+++ b/solution.py
@@ -215,51 +215,56 @@
     return jnp.concatenate(both, axis=0)
 
 
-def keep_tap(gsrc, layer, tap, h):
+def keep_taps(gsrc, layer, one):
     group = lanes((16, 128)) // 16
-    old = gsrc[layer * 4 + tap // 8] if tap % 8 else jnp.zeros((16, 128), F32)
-    gsrc[layer * 4 + tap // 8] = jnp.where(group == tap % 8, h, old)
+    tile = None
+    for tap in range(27):
+        h = one(tap // 9, tap // 3 % 3, tap % 3, tap)
+        tile = jnp.where(group == tap % 8, h, tile) if tap % 8 else h
+        if tap % 8 == 7 or tap == 26:
+            gsrc[layer * 4 + tap // 8] = tile
 
 
 def weight_gradient(src, first, cots, gsrc, layer, gtmp):
     rhs = jnp.concatenate([window(src, first + x, MID) for x in range(2)], axis=0)
     gtmp[...] = lax.dot_general(shifted_cots(cots), rhs, (((0,), (0,)), ((), ())), preferred_element_type=F32)
     group = lanes((16, 128)) // 16
-    for dx in range(3):
-        for dy in range(3):
-            for dz in range(3):
-                h = jnp.zeros((16, 128), F32)
-                extra = None
-                for zi in range(8):
-                    z = zi + dz - 1
-                    row = slice(dy * 128 + zi * 16, dy * 128 + zi * 16 + 16)
-                    if 0 <= z < 8:
-                        h = jnp.where(group == z, gtmp[row, dx * 128 : dx * 128 + 128], h)
-                    else:
-                        extra = jnp.where(group == edge_group(dx, z), gtmp[row, 384:512], 0.0)
-                if extra is not None:
-                    h = h + extra
-                for step in (64, 32, 16):
-                    h = h + pltpu.roll(h, step, 1)
-                keep_tap(gsrc, layer, 9 * dx + 3 * dy + dz, h)
+
+    def one(dx, dy, dz, tap):
+        h = jnp.zeros((16, 128), F32)
+        extra = None
+        for zi in range(8):
+            z = zi + dz - 1
+            row = slice(dy * 128 + zi * 16, dy * 128 + zi * 16 + 16)
+            if 0 <= z < 8:
+                h = jnp.where(group == z, gtmp[row, dx * 128 : dx * 128 + 128], h)
+            else:
+                extra = jnp.where(group == edge_group(dx, z), gtmp[row, 384:512], 0.0)
+        if extra is not None:
+            h = h + extra
+        for step in (64, 32, 16):
+            h = h + pltpu.roll(h, step, 1)
+        return h
+
+    keep_taps(gsrc, layer, one)
 
 
 def first_gradient(src, first, cots, gsrc, gtmp):
     rhs = jnp.concatenate([window_fields(src, first + x, MID) for x in range(2)], axis=0)
     gtmp[:, 0:128] = lax.dot_general(shifted_cots(cots), rhs, (((0,), (0,)), ((), ())), preferred_element_type=F32)
     part = lanes((16, 128)) // 4
-    for dx in range(3):
-        for dy in range(3):
-            for dz in range(3):
-                h = jnp.zeros((16, 128), F32)
-                for zi in range(8):
-                    row = slice(dy * 128 + zi * 16, dy * 128 + zi * 16 + 16)
-                    h = jnp.where(part == dx * 10 + zi + dz, gtmp[row, 0:128], h)
-                for step in (112, 120, 124):
-                    h = h + pltpu.roll(h, step, 1)
-                tap = 9 * dx + 3 * dy + dz
-                turn = ((tap % 8) * 16 - (dx * 40 + dz * 4)) % 128
-                keep_tap(gsrc, 0, tap, pltpu.roll(h, turn, 1) if turn else h)
+
+    def one(dx, dy, dz, tap):
+        h = jnp.zeros((16, 128), F32)
+        for zi in range(8):
+            row = slice(dy * 128 + zi * 16, dy * 128 + zi * 16 + 16)
+            h = jnp.where(part == dx * 10 + zi + dz, gtmp[row, 0:128], h)
+        for step in (112, 120, 124):
+            h = h + pltpu.roll(h, step, 1)
+        turn = ((tap % 8) * 16 - (dx * 40 + dz * 4)) % 128
+        return pltpu.roll(h, turn, 1) if turn else h
+
+    keep_taps(gsrc, 0, one)
 
 
 def stencil(ref, p, t, r, count, low):
@@ -424,10 +429,10 @@
     vzf[1] = vzr[0] + vzr[1]
     for copy in fc:
         copy.wait_recv()
-    vc = []
-    for place, k in ((0, 1), (1, -1)):
-        vc.append(send(vb, vbx.at[place], slab_at(k)))
-        vc.append(send(vzf.at[1], vzf.at[2 * place], slab_at(k)))
+    odd = lax.rem(s, 2)
+    pair = {"slab": s + 1 - 2 * odd}
+    beyond = {"slab": lax.rem(s + 2 - 4 * odd + SLAB, SLAB)}
+    half = [send(vb, vbx.at[odd], pair), send(vzf.at[1], vzf.at[2 * odd], pair)]
 
     def expand(src, table, dst, count, shifts, start):
         width = src.shape[2]
@@ -454,6 +459,14 @@
         @pl.loop(0, count)
         def _(p, src=src, dst=dst, k=k):
             write_plane(dst, p, jnp.tanh(conv_plane(window(src, p, ALL), wt[k])) * mask[...])
+
+        if k == 0:
+            for copy in half:
+                copy.wait_recv()
+            vc = [
+                send(vbx.at[1 - odd], vbx.at[odd], beyond),
+                send(vzf.at[2 - 2 * odd], vzf.at[2 * odd], beyond),
+            ]
 
     held[4].wait()
     held[5].wait()

time: 85.3 us -> 85.7 us (level)
  no operation moved by 1% of the time
where the time goes in v4:
time: 85.7 us; the launch traced here: 85.5 us
  Pallas kernels  84.9 us (99%)
    pallas_call x1, Pallas kernels, local(): pl.pallas_call(body, out_shape=[jax.ShapeDtypeStruct((3, 4, 144, 128), F3...  81.9 us
    pallas_call x1, Pallas kernels, local(): pl.pallas_call(finish, out_shape=[jax.ShapeDtypeStruct(*shape) for shape...  3.04 us

profile of v4, /device:TPU:1, one launch (start us, length us, event | category | flops | bytes accessed | tf_op | source)
XLA Modules:
  0.0 85.5 jit_solution(9462203962499446021)
XLA Ops:
  0.6 81.9 %shard_map.217 = (f32[3,4,144,128]{3,2,1,0:T(8,128)}, bf16[4,2,32,384]{3,2,1,0:T(8,128)(2,1)}, f32[16,16,128]{2,1,0:T(8,128)}) custom-call(f32[3,4,144,128]{3,2,1,0:T(8,128)} %v.1, bf16[3,16,27]{2,1,0:T(8,128)(2,1)} %bitcast.12, bf16[16,16,27]{2,1,0:T(8,128)(2,1)} %bitcast.9, bf16[16,16,27]{2,1,0:T(8,128)(2,1)} %bitcast.10, bf16[6,16,27]{2,1,0:T(8,128)(2,1)} %bitcast.11, ...), custom_call_target="tpu_custom_call" | custom-call | tf_op jit(solution)/shard_map/pallas_call | solution.py:688
  82.5 3.0 %shard_map.218 = (f32[3,4,144,128]{3,2,1,0:T(8,128)}, bf16[6,18,2,256]{3,2,1,0:T(2,128)(2,1)}, f32[3,16,27]{2,1,0:T(8,128)}, f32[16,16,27]{2,1,0:T(8,128)}, f32[16,16,27]{2,1,0:T(8,128)}, /*index=5*/f32[6,16,27]{2,1,0:T(8,128)}) custom-call(f32[3,4,144,128]{3,2,1,0:T(8,128)} %get-tuple-element.15.vnext, bf16[4,2,32,384]{3,2,1,0:T(8,128)(2,1)} %get-tuple-element.16.sw, ...), custom_call_target="tpu_custom_call" | custom-call | tf_op jit(solution)/shard_map/pallas_call | solution.py:710
